TPU v7x, 768 devices: a whole 4x8x12 slice. The times are simulated.
768 devices in a mesh: row: 16 (over y_lo, x, core), col: 48 (over y_hi, z).
Axes of the slice: x: 4, y: 8 (y_hi: 4, y_lo: 2; y = y_hi * 2 + y_lo), z: 12, core: 2. Of those that a mesh axis runs over, the one named last changes fastest.
Arguments:
- features: bfloat16 [98304, 128], P(('col', 'row')), may hold values from -6 to 6
- weight: bfloat16 [128, 256], replicated, may hold values from -0.5 to 0.5
- out_bias: float32 [256], replicated, may hold values from -3 to 3
- tile_values: bfloat16 [16, 48, 64, 128, 128], P('row', 'col'), may hold values from -0.0625 to 0.0625
- tile_rows: int32 [16, 48, 64], P('row', 'col'), may hold values from 0 to 47
- band_offsets: int32 [16, 48, 64], P('row', 'col'), may hold values from -4 to 4
- tile_count: int32 [16, 48], P('row', 'col'), may hold values from 8 to 64, as said below
- cotangent: bfloat16 [98304, 256], P(('row', 'col')), may hold values from -6 to 6
Outputs:
- activated: bfloat16 [98304, 256], P(('row', 'col'))
- feature_grad: bfloat16 [98304, 128], P(('col', 'row'))
- weight_grad: float32 [128, 256], replicated
- bias_grad: float32 [256], replicated
Inputs may be any that keep to these rules, and one draw needn't show every extreme that they name: `tile_count`: the live slots of a device are its first ones; some device has all 64 slots live in every draw.
All inputs are finite; a program needn't handle non-finite values.
Results may differ from a plain program's by a relative error of at most 0.011.
Values may be sent and summed in bfloat16 or wider, within the bound.
No kernel may reach another device: no remote copies, remote signals or barrier semaphores. Data moves between devices by JAX's collectives and lax.ppermute only.
A program may use at most 32 MiB of HBM per device.

v0:
```python
import math

import jax
import jax.numpy as jnp
from jax import lax
from jax.sharding import PartitionSpec as P


def add_products(
    running, values_blk, rows_blk, source_blk, first_slot, lower_end, upper_end, first_tile
):
    span_tiles = running.shape[0]
    index_list = first_slot + jnp.arange(values_blk.shape[0], dtype=jnp.int32)
    local_rows = rows_blk - first_tile
    inside = (local_rows >= 0) & (local_rows < span_tiles)
    kept = ((index_list >= lower_end) & (index_list < upper_end) & inside).astype(jnp.float32)
    product = jnp.einsum("kij,kjf->kif", values_blk, source_blk, preferred_element_type=jnp.float32)
    placed = jnp.clip(local_rows, 0, span_tiles - 1)
    return running.at[placed].add(product * kept[:, None, None])


def backward_sweep(values_all, rows_all, cols_all, live_total, source_parts, col_tiles):
    first_part = source_parts[0]
    width_out = first_part.shape[-1]
    start_back = jnp.zeros((col_tiles, first_part.shape[1], width_out), jnp.float32)

    def back_turn(block_num, running):
        first_slot = block_num * 8
        values_blk = lax.dynamic_slice_in_dim(values_all, first_slot, 8, 0)
        rows_blk = lax.dynamic_slice_in_dim(rows_all, first_slot, 8, 0)
        cols_blk = lax.dynamic_slice_in_dim(cols_all, first_slot, 8, 0)
        product = jnp.zeros((8, first_part.shape[1], width_out), jnp.float32)
        for part_tiles in source_parts:
            source_blk = jnp.take(part_tiles, rows_blk, axis=0)
            product = product + jnp.einsum(
                "kij,kif->kjf", values_blk, source_blk, preferred_element_type=jnp.float32
            )
        kept = (first_slot + jnp.arange(8, dtype=jnp.int32) < live_total).astype(jnp.float32)
        return running.at[cols_blk].add(product * kept[:, None, None])

    return lax.fori_loop(0, (live_total + 7) // 8, back_turn, start_back)


def local(features, weight, out_bias, tile_values, tile_rows, band_offsets, tile_count, cotangent):
    tile_size = tile_values.shape[-1]
    width_in = features.shape[1]
    local_nodes = features.shape[0]
    row_tiles = local_nodes * lax.axis_size("col") // tile_size
    col_tiles = local_nodes * lax.axis_size("row") // tile_size
    values_all = tile_values[0, 0]
    rows_all = tile_rows[0, 0]
    cols_all = (rows_all * col_tiles // row_tiles + band_offsets[0, 0]) % col_tiles
    live_total = tile_count[0, 0]
    panel = lax.all_gather(features, "row", axis=0, tiled=True)
    panel_tiles = panel.reshape(col_tiles, tile_size, width_in)
    running = jnp.zeros((row_tiles, tile_size, width_in), jnp.float32)

    def own_turn(block_num, partial_sum):
        first_slot = block_num * 8
        values_blk = lax.dynamic_slice_in_dim(values_all, first_slot, 8, 0)
        rows_blk = lax.dynamic_slice_in_dim(rows_all, first_slot, 8, 0)
        cols_blk = lax.dynamic_slice_in_dim(cols_all, first_slot, 8, 0)
        source_blk = jnp.take(panel_tiles, cols_blk, axis=0)
        return add_products(
            partial_sum, values_blk, rows_blk, source_blk, first_slot, 0, live_total, 0
        )

    running = lax.fori_loop(0, (live_total + 7) // 8, own_turn, running)
    aggregated = lax.psum_scatter(
        running.reshape(row_tiles * tile_size, width_in), "col", scatter_dimension=0, tiled=True
    )
    preact = (
        jnp.dot(aggregated, weight.astype(jnp.float32), precision=lax.Precision.HIGHEST) + out_bias
    )
    sigmoid = jax.nn.sigmoid(preact)
    activated = (preact * sigmoid).astype(jnp.bfloat16)
    grad_pre = (cotangent.astype(jnp.float32) * sigmoid * (1.0 + preact * (1.0 - sigmoid))).astype(
        jnp.bfloat16
    )
    grad_float = grad_pre.astype(jnp.float32)
    local_wgrad = jnp.dot(aggregated.T, grad_float, precision=lax.Precision.HIGHEST)
    local_bgrad = jnp.sum(grad_float, axis=0)
    summed_wgrad, summed_bgrad = lax.psum((local_wgrad, local_bgrad), ("row", "col"))
    factor = 1.0 / math.sqrt(local_nodes * lax.axis_size("row") * lax.axis_size("col"))
    weight_grad = summed_wgrad * factor
    bias_grad = summed_bgrad * factor
    projected = jnp.dot(grad_pre, weight.T, preferred_element_type=jnp.float32)
    target_panel = lax.all_gather(projected, "col", axis=0, tiled=True)
    target_tiles = target_panel.reshape(row_tiles, tile_size, width_in)
    upper_part = target_tiles.astype(jnp.bfloat16)
    lower_part = (target_tiles - upper_part.astype(jnp.float32)).astype(jnp.bfloat16)
    back_sum = backward_sweep(
        values_all, rows_all, cols_all, live_total, (upper_part, lower_part), col_tiles
    )
    summed = lax.psum_scatter(
        back_sum.reshape(col_tiles * tile_size, width_in), "row", scatter_dimension=0, tiled=True
    )
    feature_grad = summed.astype(jnp.bfloat16)
    return (activated, feature_grad, weight_grad, bias_grad)


def solution(mesh):
    placed = (
        P(("col", "row"), None),
        P(),
        P(),
        P("row", "col", None, None, None),
        P("row", "col", None),
        P("row", "col", None),
        P("row", "col"),
        P(("row", "col"), None),
    )
    return jax.shard_map(
        local,
        mesh=mesh,
        in_specs=placed,
        out_specs=(P(("row", "col"), None), P(("col", "row"), None), P(), P()),
        check_vma=False,
    )
```

profile of v0, /device:TPU:1, one launch (start us, length us, event | category | flops | bytes accessed | tf_op | source)
XLA Modules:
  0.0 1167.7 jit_solution(6039327051437265583)
XLA Ops:
  8.1 28.1 %all_gather.6 = bf16[2048,128]{1,0:T(8,128)(2,1)S(1)} all-gather(bf16[128,128]{1,0:T(8,128)(2,1)} %param.14), channel_id=1, replica_groups=mesh['row'=16,'col'=48] {'row'}, dimensions={0}, use_global_device_ids=true | all-gather | bytes 557056 | tf_op jit(solution)/shard_map/all_gather | solution.py:54
  36.9 2.0 broadcast_in_dim.36
  38.9 17.7 %while.20 = (s32[]{:T(128)}, f32[48,128,128]{2,1,0:T(8,128)}, s32[]{:T(128)}, s32[64]{0:T(128)S(1)}, bf16[64,128,128]{2,1,0:T(8,128)(2,1)S(1)}, /*index=5*/s32[6...) while((s32[]{:T(128)}, f32[48,128,128]{2,1,0:T(8,128)}, ...), condition=%wide.region_2.3_spmd, body=%wide.region_0.2_spmd.sunk | while | flops 33948828 | bytes 3151327 | solution.py:68
  38.9 0.7 compare_and_fusion.4
  40.6 2.7 scatter_fusion
  43.3 0.7 compare_and_fusion.4
  45.1 2.7 scatter_fusion
  49.5 2.7 scatter_fusion
  52.2 0.7 compare_and_fusion.4
  53.9 2.7 scatter_fusion
  56.7 446.5 %reduce-scatter.3.cloned.1.call-done = f32[128,128]{1,0:T(8,128)} async-done(((f32[6144,128]{1,0:T(8,128)}), f32[128,128]{1,0:T(8,128)}) %reduce-scatter.3.cloned.1.call-update) | async-done | bytes 65552 | tf_op jit(solution)/shard_map/reduce_scatter | solution.py:69
  503.2 1.7 convert_reduce_fusion
  504.9 0.8 fusion.21
  505.7 2.9 copy.12
  508.7 0.9 fusion.22
  509.6 119.7 %all-gather.2.cloned.1.call-done = f32[6144,128]{1,0:T(8,128)} async-done(((f32[128,128]{1,0:T(8,128)}), f32[6144,128]{1,0:T(8,128)}) %all-gather.2.cloned.1.call-update) | async-done | bytes 3145744 | tf_op jit(solution)/shard_map/all_gather | solution.py:88
  629.4 5.4 subtract_convert_fusion
  634.9 33.7 %while.21 = (s32[]{:T(128)}, f32[16,128,128]{2,1,0:T(8,128)S(1)}, s32[]{:T(128)}, s32[64]{0:T(128)S(1)}, bf16[64,128,128]{1,2,0:T(8,128)(2,1)}, /*index=5*/s32[6...) while((s32[]{:T(128)}, f32[16,128,128]{2,1,0:T(8,128)S(1)}, ...), condition=%wide.region_6.8_spmd, body=%wide.region_4.7_spmd.sunk | while | flops 67765344 | bytes 5247515 | solution.py:41
  634.9 0.7 compare_and_fusion.5
  635.6 2.0 gather_fusion.1
  637.7 1.3 fusion.43
  638.9 2.0 gather_fusion.2
  640.9 1.3 fusion.44
  642.3 1.0 scatter_fusion.1
  643.3 0.7 compare_and_fusion.5
  644.1 2.0 gather_fusion.1
  646.1 1.3 fusion.43
  647.3 2.0 gather_fusion.2
  649.3 1.3 fusion.44
  650.7 1.0 scatter_fusion.1
  651.7 0.7 compare_and_fusion.5
  652.5 2.0 gather_fusion.1
  654.5 1.2 fusion.43
  655.8 2.0 gather_fusion.2
  657.8 1.3 fusion.44
  659.1 1.0 scatter_fusion.1
  660.2 0.7 compare_and_fusion.5
  660.9 2.0 gather_fusion.1
  662.9 1.3 fusion.43
  664.2 2.0 gather_fusion.2
  666.2 1.3 fusion.44
  667.5 1.0 scatter_fusion.1
  668.6 1.0 copy-done.1
  669.6 146.2 %psum.15 = f32[256]{0:T(256)S(1)} all-reduce(f32[256]{0:T(256)S(1)} %get-tuple-element.144), channel_id=1, replica_groups=mesh['row'=16,'col'=48] {'row','col'}, use_global_device_ids=true, to_apply=%region_10.12 | all-reduce | flops 256 | bytes 2048 | tf_op jit(solution)/shard_map/psum | solution.py:83
  816.4 276.9 %all-reduce.2.cloned.1.call-done = f32[128,256]{1,0:T(8,128)} async-done(((f32[128,256]{1,0:T(8,128)}), f32[128,256]{1,0:T(8,128)}) %all-reduce.2.cloned.1.call-update) | async-done | bytes 131088 | tf_op jit(solution)/shard_map/psum | solution.py:83
  1093.2 1.6 broadcast_multiply_fusion
  1094.8 64.9 %reduce-scatter.5.cloned.1.call-done = f32[128,128]{1,0:T(8,128)} async-done(((f32[2048,128]{1,0:T(8,128)}), f32[128,128]{1,0:T(8,128)}) %reduce-scatter.5.cloned.1.call-update) | async-done | bytes 65552 | tf_op jit(solution)/shard_map/reduce_scatter | solution.py:95
  1159.7 1.5 convert_element_type.41
  (49 shorter events, 6.6 us)
Async XLA Ops:
  7.2 496.0 %copy-start = (bf16[128,256]{1,0:T(8,128)(2,1)S(1)}, bf16[128,256]{1,0:T(8,128)(2,1)}, u32[]{:S(2)}) copy-start(bf16[128,256]{1,0:T(8,128)(2,1)} %param.15) | copy-start | bytes 196612
  7.2 31.7 %copy-start.4 = (s32[1,1,64]{2,1,0:T(1,128)S(1)}, s32[1,1,64]{2,1,0:T(1,128)}, u32[]{:S(2)}) copy-start(s32[1,1,64]{2,1,0:T(1,128)} %param.18) | copy-start | bytes 772
  7.2 31.7 %copy-start.2 = (bf16[1,1,64,128,128]{4,3,2,1,0:T(8,128)(2,1)S(1)}, bf16[1,1,64,128,128]{4,3,2,1,0:T(8,128)(2,1)}, u32[]{:S(2)}) copy-start(bf16[1,1,64,128,128]{4,3,2,1,0:T(8,128)(2,1)} %param.17) | copy-start | bytes 6291460
  7.2 495.9 %reduce-scatter.3.cloned.1.call-start = ((), (), s32[]{:S(2)}) async-start(), calls=%async_computation.2 | async-start | bytes 3211264 | tf_op jit(solution)/shard_map/reduce_scatter | solution.py:69
  56.6 446.5 %copy-start.5 = (bf16[128,256]{1,0:T(8,128)(2,1)S(1)}, bf16[128,256]{1,0:T(8,128)(2,1)}, u32[]{:S(2)}) copy-start(bf16[128,256]{1,0:T(8,128)(2,1)} %param.21) | copy-start | bytes 196612
  56.6 446.5 %copy-start.6 = (f32[256]{0:T(256)S(1)}, f32[256]{0:T(256)}, u32[]{:S(2)}) copy-start(f32[256]{0:T(256)} %param.16) | copy-start | bytes 3076
  56.6 572.7 %all-gather.2.cloned.1.call-start = ((), (), s32[]{:S(2)}) async-start(), calls=%async_computation.3 | async-start | bytes 3211264 | tf_op jit(solution)/shard_map/all_gather | solution.py:88
  505.7 3.0 copy-start.3
  505.7 587.6 %all-reduce.2.cloned.1.call-start = ((), (), s32[]{:S(2)}) async-start(), calls=%async_computation.5 | async-start | bytes 262144 | tf_op jit(solution)/shard_map/psum | solution.py:83
  509.6 650.1 %reduce-scatter.5.cloned.1.call-start = ((), (), s32[]{:S(2)}) async-start(), calls=%async_computation.4 | async-start | bytes 1114112 | tf_op jit(solution)/shard_map/reduce_scatter | solution.py:95
  668.6 1.0 copy-start.1
Sparse Core Ops, SparseCore 0:
  56.8 446.3 reduce-scatter.2
  506.7 122.5 all-gather.1
  635.3 457.8 all-reduce.1
  1096.5 63.1 reduce-scatter.4
where the time goes:
time: 1170 us
  waiting for transfers between devices  908 us (78%)
  blocking collectives  174 us (15%)
  other arithmetic  31.1 us (3%)
  local copies, waits for them, and re-layouts  24.5 us (2%)
  matrix products  14.6 us (1%)
  between operations  14.6 us (1%)
    reduce_scatter x1, waiting for transfers between devices, local(): lax.psum_scatter(running.reshape(row_tiles * tile_size, width_in), 'col',...  446 us
    psum x1, waiting for transfers between devices, local(): lax.psum((local_wgrad, local_bgrad), ('row', 'col'))  277 us
    psum x1, blocking collectives, local(): lax.psum((local_wgrad, local_bgrad), ('row', 'col'))  146 us
    all_gather x1, waiting for transfers between devices, local(): target_panel = lax.all_gather(projected, 'col', axis=0, tiled=True)  120 us
    reduce_scatter x1, waiting for transfers between devices, local(): lax.psum_scatter(back_sum.reshape(col_tiles * tile_size, width_in), 'row'...  64.9 us
    all_gather x1, blocking collectives, local(): panel = lax.all_gather(features, 'row', axis=0, tiled=True)  28.1 us
  transfers between devices with their start and end apart: 4, of which 4 were waited for; matrix products, arithmetic and copies ran while one was open for 4% of the time, Pallas kernels for 0%

commit v1 on v0

v1 whole, which is shorter than its diff:
```python
import functools
import math

import jax
import jax.numpy as jnp
from jax import lax
from jax.experimental import pallas as pl
from jax.experimental.pallas import tpu as pltpu
from jax.sharding import PartitionSpec as P

TILE = 128
FIN = 128
HID = 256
CAP = 64
RT = 48
CT = 16
STEP = 8
EXTRA = 32
SHARE = 24

SMEM = pl.BlockSpec(memory_space=pltpu.SMEM)
VMEM = pl.BlockSpec(memory_space=pltpu.VMEM)
LIMIT = pltpu.CompilerParams(vmem_limit_bytes=32 * 1024 * 1024)


def dot(a, b, dims=((1,), (0,))):
    return lax.dot_general(a, b, (dims, ((), ())), preferred_element_type=jnp.float32)


def forward_kernel(dst_ref, src_ref, blocks_ref, values_ref, panel_ref, out_ref, acc_ref):
    acc_ref[...] = jnp.zeros_like(acc_ref)

    def step(block, carry):
        for offset in range(STEP):
            k = block * STEP + offset
            product = dot(values_ref[k], panel_ref[src_ref[k]])
            acc_ref[dst_ref[k]] += product
        return carry

    lax.fori_loop(0, blocks_ref[0], step, 0)
    out_ref[...] = acc_ref[:RT].astype(jnp.bfloat16)


def forward(dst, src, blocks, values, panel):
    return pl.pallas_call(
        forward_kernel,
        out_shape=jax.ShapeDtypeStruct((RT, TILE, FIN), jnp.bfloat16),
        in_specs=[SMEM, SMEM, SMEM, VMEM, VMEM],
        out_specs=VMEM,
        scratch_shapes=[pltpu.VMEM((RT + 1, TILE, FIN), jnp.float32)],
        compiler_params=LIMIT,
    )(dst, src, blocks, values, panel)


def local_kernel(parts_ref, cot_ref, weight_ref, bias_ref, act_ref, proj_ref, grads_ref):
    def add(i, total):
        return total + parts_ref[i].astype(jnp.float32)

    agg = lax.fori_loop(1, parts_ref.shape[0], add, parts_ref[0].astype(jnp.float32), unroll=True)
    upper = agg.astype(jnp.bfloat16)
    lower = (agg - upper.astype(jnp.float32)).astype(jnp.bfloat16)
    weight = weight_ref[...]
    preact = dot(upper, weight) + dot(lower, weight) + bias_ref[...]
    sigmoid = 1.0 / (1.0 + jnp.exp(-preact))
    act_ref[...] = (preact * sigmoid).astype(jnp.bfloat16)
    cot = cot_ref[...].astype(jnp.float32)
    grad = (cot * sigmoid * (1.0 + preact * (1.0 - sigmoid))).astype(jnp.bfloat16)
    proj_ref[...] = dot(weight, grad, ((1,), (1,))).astype(jnp.bfloat16)
    over_nodes = ((0,), (0,))
    wgrad = dot(upper, grad, over_nodes) + dot(lower, grad, over_nodes)
    bgrad = jnp.sum(grad.astype(jnp.float32), axis=0, keepdims=True)
    rows = FIN // 8
    for j in range(8):
        grads_ref[j, :rows, :] = wgrad[j * rows : (j + 1) * rows, :FIN]
        grads_ref[8 + j, :rows, :] = wgrad[j * rows : (j + 1) * rows, FIN:]
    tail = jnp.concatenate(
        [bgrad[:, :FIN], bgrad[:, FIN:], jnp.zeros((SHARE - rows - 2, FIN), jnp.float32)], axis=0
    )
    for j in range(16):
        grads_ref[j, rows:, :] = tail


def local_part(parts, cot, weight, bias):
    return pl.pallas_call(
        local_kernel,
        out_shape=(
            jax.ShapeDtypeStruct((TILE, HID), jnp.bfloat16),
            jax.ShapeDtypeStruct((FIN, TILE), jnp.bfloat16),
            jax.ShapeDtypeStruct((CT, SHARE, FIN), jnp.float32),
        ),
        in_specs=[VMEM] * 4,
        out_specs=(VMEM, VMEM, VMEM),
        compiler_params=LIMIT,
    )(parts, cot, weight, bias)


def backward_kernel(dst_ref, src_ref, blocks_ref, values_ref, panel_ref, out_ref, acc_ref):
    acc_ref[...] = jnp.zeros_like(acc_ref)

    def step(block, carry):
        for offset in range(STEP):
            k = block * STEP + offset
            product = dot(panel_ref[src_ref[k], :TILE, :], values_ref[k])
            acc_ref[dst_ref[k]] += product
        return carry

    lax.fori_loop(0, blocks_ref[0], step, 0)
    out_ref[:, :TILE, :] = acc_ref[:CT].astype(jnp.bfloat16)
    share = panel_ref[0, TILE:, :].astype(jnp.float32)
    for i in range(1, panel_ref.shape[0]):
        share = share + panel_ref[i, TILE:, :].astype(jnp.float32)
    share = share.astype(jnp.bfloat16)
    for j in range(CT):
        out_ref[j, TILE:, :] = share


def backward(dst, src, blocks, values, panel):
    return pl.pallas_call(
        backward_kernel,
        out_shape=jax.ShapeDtypeStruct((CT, TILE + EXTRA, TILE), jnp.bfloat16),
        in_specs=[SMEM, SMEM, SMEM, VMEM, VMEM],
        out_specs=VMEM,
        scratch_shapes=[pltpu.VMEM((CT + 1, TILE, TILE), jnp.float32)],
        compiler_params=LIMIT,
    )(dst, src, blocks, values, panel)


def final_kernel(factor, parts_ref, feature_ref, wgrad_ref, bgrad_ref):
    total = parts_ref[0, :TILE, :].astype(jnp.float32)
    for i in range(1, CT):
        total = total + parts_ref[i, :TILE, :].astype(jnp.float32)
    feature_ref[...] = total.T.astype(jnp.bfloat16)
    rows = FIN // 8
    for j in range(8):
        left = parts_ref[j, TILE : TILE + rows, :].astype(jnp.float32) * factor
        right = parts_ref[8 + j, TILE : TILE + rows, :].astype(jnp.float32) * factor
        wgrad_ref[j * rows : (j + 1) * rows, :FIN] = left
        wgrad_ref[j * rows : (j + 1) * rows, FIN:] = right
    tail = parts_ref[0, TILE + rows :, :].astype(jnp.float32) * factor
    bgrad_ref[:, :FIN] = tail[0:1]
    bgrad_ref[:, FIN:] = tail[1:2]


def final_part(parts, factor):
    return pl.pallas_call(
        functools.partial(final_kernel, factor),
        out_shape=(
            jax.ShapeDtypeStruct((TILE, FIN), jnp.bfloat16),
            jax.ShapeDtypeStruct((FIN, HID), jnp.float32),
            jax.ShapeDtypeStruct((1, HID), jnp.float32),
        ),
        in_specs=[VMEM],
        out_specs=(VMEM, VMEM, VMEM),
        compiler_params=LIMIT,
    )(parts)


def local(features, weight, out_bias, tile_values, tile_rows, band_offsets, tile_count, cotangent):
    values = tile_values[0, 0]
    rows = tile_rows[0, 0]
    cols = (rows * CT // RT + band_offsets[0, 0]) % CT
    live = jnp.arange(CAP, dtype=jnp.int32) < tile_count[0, 0]
    blocks = (tile_count[0] + STEP - 1) // STEP
    panel = lax.all_to_all(
        jnp.broadcast_to(features, (CT, TILE, FIN)), "row", 0, 0, tiled=True
    )
    partial = forward(jnp.where(live, rows, RT), cols, blocks, values, panel)
    parts = lax.all_to_all(partial, "col", 0, 0, tiled=True)
    activated, proj, grads = local_part(parts, cotangent, weight, out_bias.reshape(1, HID))
    grads = lax.all_to_all(grads, "row", 0, 0, tiled=True)
    share = jnp.sum(grads, axis=0).astype(jnp.bfloat16)
    block = jnp.concatenate([proj, share, jnp.zeros((EXTRA - SHARE, FIN), jnp.bfloat16)], axis=0)
    targets = lax.all_to_all(
        jnp.broadcast_to(block, (RT, TILE + EXTRA, TILE)), "col", 0, 0, tiled=True
    )
    back = backward(jnp.where(live, cols, CT), rows, blocks, values, targets)
    back = lax.all_to_all(back, "row", 0, 0, tiled=True)
    nodes = TILE * lax.axis_size("row") * lax.axis_size("col")
    feature_grad, weight_grad, bias_grad = final_part(back, 1.0 / math.sqrt(nodes))
    return (activated, feature_grad, weight_grad, bias_grad.reshape(HID))


def solution(mesh):
    placed = (
        P(("col", "row"), None),
        P(),
        P(),
        P("row", "col", None, None, None),
        P("row", "col", None),
        P("row", "col", None),
        P("row", "col"),
        P(("row", "col"), None),
    )
    return jax.shard_map(
        local,
        mesh=mesh,
        in_specs=placed,
        out_specs=(P(("row", "col"), None), P(("col", "row"), None), P(), P()),
        check_vma=False,
    )
```

time: 1170 us -> 219 us (0.19)
  waiting for transfers between devices: 908 us -> 15.1 us
  other arithmetic: 31.1 us -> 0.8 us
  starting transfers between devices: 0.16 us -> 22.3 us
  local copies, waits for them, and re-layouts: 24.5 us -> 3.61 us
  matrix products: 14.6 us -> 0 us
  between operations: 14.6 us -> 1.39 us
    reduce_scatter x2 -> x0, waiting for transfers between devices: 511 us -> none  [the longest x1 446 us: local(): lax.psum_scatter(running.reshape(row_tiles * tile_size, width_in), 'col',...]
    psum x1 -> x0, waiting for transfers between devices: 277 us -> none  [local(): lax.psum((local_wgrad, local_bgrad), ('row', 'col'))]
    all_to_all x0 -> x3, blocking collectives: none -> 169 us  [the longest x1 80.6 us: local(): lax.all_to_all(jnp.broadcast_to(block, (RT, TILE + EXTRA, TILE)), 'col',...]
    psum x1 -> x0, blocking collectives: 146 us -> none  [local(): lax.psum((local_wgrad, local_bgrad), ('row', 'col'))]
    all_gather x1 -> x0, waiting for transfers between devices: 120 us -> none  [local(): target_panel = lax.all_gather(projected, 'col', axis=0, tiled=True)]
    all_gather x1 -> x0, blocking collectives: 28.1 us -> none  [local(): panel = lax.all_gather(features, 'row', axis=0, tiled=True)]
    all_to_all x0 -> x2, starting transfers between devices: none -> 22.3 us  [the longest x1 13.9 us: local(): lax.all_to_all(jnp.broadcast_to(features, (CT, TILE, FIN)), 'row', 0, 0,...]
    gather x12 -> x0, local copies, waits for them, and re-layouts: 18.5 us -> none  [the longest x8 16.1 us: back_turn(): source_blk = jnp.take(part_tiles, rows_blk, axis=0)]
  transfers between devices with their start and end apart: 4 -> 2, of which waited for: 4 -> 2; matrix products, arithmetic and copies ran while one was open for 4% -> 0% of each run, Pallas kernels for 0% -> 0%
where the time goes in v1:
time: 219 us; the launch traced here: 218 us
  blocking collectives  169 us (77%)
  starting transfers between devices  22.3 us (10%)
  waiting for transfers between devices  15.1 us (7%)
  Pallas kernels  6.08 us (3%)
  local copies, waits for them, and re-layouts  3.61 us (2%)
    all_to_all x1, blocking collectives, local(): lax.all_to_all(jnp.broadcast_to(block, (RT, TILE + EXTRA, TILE)), 'col',...  80.6 us
    all_to_all x1, blocking collectives, local(): parts = lax.all_to_all(partial, 'col', 0, 0, tiled=True)  68.2 us
    all_to_all x1, blocking collectives, local(): back = lax.all_to_all(back, 'row', 0, 0, tiled=True)  20 us
    all_to_all x1, starting transfers between devices, local(): lax.all_to_all(jnp.broadcast_to(features, (CT, TILE, FIN)), 'row', 0, 0,...  13.9 us
    all_to_all x1, waiting for transfers between devices, local(): lax.all_to_all(jnp.broadcast_to(features, (CT, TILE, FIN)), 'row', 0, 0,...  8.51 us
    all_to_all x1, starting transfers between devices, local(): grads = lax.all_to_all(grads, 'row', 0, 0, tiled=True)  8.42 us
    all_to_all x1, waiting for transfers between devices, local(): grads = lax.all_to_all(grads, 'row', 0, 0, tiled=True)  6.6 us
  transfers between devices with their start and end apart: 2, of which 2 were waited for; matrix products, arithmetic and copies ran while one was open for 0% of the time, Pallas kernels for 0%

profile of v1, /device:TPU:1, one launch (start us, length us, event | category | flops | bytes accessed | tf_op | source)
XLA Modules:
  0.0 218.1 jit_solution(7107483086422785602)
XLA Ops:
  0.6 1.7 broadcast_in_dim.15
  2.3 13.9 %all-to-all-start = ((bf16[16,128,128]{2,1,0:T(8,128)(2,1)}), bf16[16,128,128]{2,1,0:T(8,128)(2,1)S(1)}, u32[]{:S(2)}, u32[]{:S(2)}) async-start(bf16[16,128,128]{2,1,0:T(8,128)(2,1)} %broadcast_in_dim.15), calls=%async_computation | async-start | bytes 1048576 | tf_op jit(solution)/shard_map/all_to_all | solution.py:164
  16.8 0.7 compare_select_fusion.2
  17.5 8.5 %all-to-all-done.panel_ref = bf16[16,128,128]{2,1,0:T(8,128)(2,1)S(1)} async-done(((bf16[16,128,128]{2,1,0:T(8,128)(2,1)}), bf16[16,128,128]{2,1,0:T(8,128)(2,1)S(1)}, u32[]{:S(2)}, u32[]{:S(2)}) %all-to-all-start) | async-done | bytes 524320 | tf_op jit(solution)/shard_map/all_to_all | solution.py:164
  26.0 0.0 copy-start
  26.0 1.6 copy-done
  27.6 2.1 shard_map.111
  29.7 0.0 copy-start.2
  29.7 0.0 copy-start.3
  29.8 0.0 copy-start.5
  29.8 68.2 %all_to_all.25.parts_ref = bf16[48,128,128]{2,1,0:T(8,128)(2,1)S(1)} all-to-all(bf16[48,128,128]{2,1,0:T(8,128)(2,1)S(1)} %shard_map.111), channel_id=1, replica_groups=mesh['row'=16,'col'=48] {'col'}, dimensions={0} | all-to-all | bytes 3145728 | tf_op jit(solution)/shard_map/all_to_all | solution.py:168
  98.0 0.0 copy-done.2
  98.0 0.0 copy-done.3
  98.0 0.0 copy-done.5
  98.0 1.3 shard_map.112
  99.3 8.4 %all-to-all-start.2 = ((f32[16,24,128]{2,1,0:T(8,128)}), f32[16,24,128]{2,1,0:T(8,128)S(1)}, u32[]{:S(2)}, u32[]{:S(2)}) async-start(f32[16,24,128]{2,1,0:T(8,128)} %get-tuple-element.12), calls=%async_computation.2 | async-start | bytes 393216 | tf_op jit(solution)/shard_map/all_to_all | solution.py:170
  107.7 0.1 pad.2.clone
  107.8 6.6 %all-to-all-done.2 = f32[16,24,128]{2,1,0:T(8,128)S(1)} async-done(((f32[16,24,128]{2,1,0:T(8,128)}), f32[16,24,128]{2,1,0:T(8,128)S(1)}, u32[]{:S(2)}, u32[]{:S(2)}) %all-to-all-start.2) | async-done | bytes 196640 | tf_op jit(solution)/shard_map/all_to_all | solution.py:170
  114.4 0.1 maximum_maximum_fusion
  114.5 0.3 broadcast_in_dim.17
  114.8 0.0 copy-start.1
  114.8 0.0 copy-start.4
  114.8 80.6 %all_to_all.26.panel_ref = bf16[48,160,128]{2,1,0:T(8,128)(2,1)S(1)} all-to-all(bf16[48,160,128]{2,1,0:T(8,128)(2,1)S(1)} %broadcast_in_dim.17), channel_id=1, replica_groups=mesh['row'=16,'col'=48] {'col'}, dimensions={0} | all-to-all | bytes 3932160 | tf_op jit(solution)/shard_map/all_to_all | solution.py:173
  195.4 0.0 copy-done.1
  195.4 0.0 copy-done.4
  195.4 1.9 shard_map.113
  197.4 20.0 %all_to_all.27.parts_ref = bf16[16,160,128]{2,1,0:T(8,128)(2,1)S(1)} all-to-all(bf16[16,160,128]{2,1,0:T(8,128)(2,1)S(1)} %shard_map.113), channel_id=1, replica_groups=mesh['row'=16,'col'=48] {'row'}, dimensions={0} | all-to-all | bytes 1310720 | tf_op jit(solution)/shard_map/all_to_all | solution.py:177
  217.3 0.8 shard_map.114
  (2 shorter events, 0.0 us)
Async XLA Ops:
  2.3 23.8 %all-to-all-start = ((bf16[16,128,128]{2,1,0:T(8,128)(2,1)}), bf16[16,128,128]{2,1,0:T(8,128)(2,1)S(1)}, u32[]{:S(2)}, u32[]{:S(2)}) async-start(bf16[16,128,128]{2,1,0:T(8,128)(2,1)} %broadcast_in_dim.15), calls=%async_computation | async-start | bytes 1048576 | tf_op jit(solution)/shard_map/all_to_all | solution.py:164
  26.0 1.6 copy-start
  29.7 68.3 %copy-start.2 = (bf16[128,256]{1,0:T(8,128)(2,1)S(1)}, bf16[128,256]{1,0:T(8,128)(2,1)}, u32[]{:S(2)}) copy-start(bf16[128,256]{1,0:T(8,128)(2,1)} %cot_ref.1) | copy-start | bytes 196612
  29.7 68.2 %copy-start.3 = (bf16[128,256]{1,0:T(8,128)(2,1)S(1)}, bf16[128,256]{1,0:T(8,128)(2,1)}, u32[]{:S(2)}) copy-start(bf16[128,256]{1,0:T(8,128)(2,1)} %weight_ref.1) | copy-start | bytes 196612
  29.8 68.2 %copy-start.5 = (f32[256]{0:T(256)S(1)}, f32[256]{0:T(256)}, u32[]{:S(2)}) copy-start(f32[256]{0:T(256)} %param.10) | copy-start | bytes 3076
  99.3 15.1 %all-to-all-start.2 = ((f32[16,24,128]{2,1,0:T(8,128)}), f32[16,24,128]{2,1,0:T(8,128)S(1)}, u32[]{:S(2)}, u32[]{:S(2)}) async-start(f32[16,24,128]{2,1,0:T(8,128)} %get-tuple-element.12), calls=%async_computation.2 | async-start | bytes 393216 | tf_op jit(solution)/shard_map/all_to_all | solution.py:170
  114.8 80.6 %copy-start.1 = (bf16[1,1,64,128,128]{4,3,2,1,0:T(8,128)(2,1)S(1)}, bf16[1,1,64,128,128]{4,3,2,1,0:T(8,128)(2,1)}, u32[]{:S(2)}) copy-start(bf16[1,1,64,128,128]{4,3,2,1,0:T(8,128)(2,1)} %param.11) | copy-start | bytes 6291460
  114.8 80.6 %copy-start.4 = (s32[1,1,64]{2,1,0:T(1,128)S(1)}, s32[1,1,64]{2,1,0:T(1,128)}, u32[]{:S(2)}) copy-start(s32[1,1,64]{2,1,0:T(1,128)} %param.12) | copy-start | bytes 772

commit v2 on v1

v2 whole, which is shorter than its diff:
```python
import functools
import math

import jax
import jax.numpy as jnp
from jax import lax
from jax.experimental import pallas as pl
from jax.experimental.pallas import tpu as pltpu
from jax.sharding import Mesh
from jax.sharding import PartitionSpec as P

TILE = 128
FIN = 128
HID = 256
CAP = 64
RT = 48
CT = 16
STEP = 8
EXTRA = 32
SHARE = 24
NEAR = 4
FAR = RT // NEAR
HALF = FAR // 2
DEPTH = 12
STAGES = 5

ROW = ("yl", "x", "core")
COL = ("yh", "za", "zb")
GROUP = ("yh", "za")
LINE = ("za", "zb")

SMEM = pl.BlockSpec(memory_space=pltpu.SMEM)
VMEM = pl.BlockSpec(memory_space=pltpu.VMEM)
LIMIT = pltpu.CompilerParams(vmem_limit_bytes=32 * 1024 * 1024)
def shift(block, steps):
    return lax.ppermute(block, LINE, [(z, (z + steps) % DEPTH) for z in range(DEPTH)])


def dot(a, b, dims=((1,), (0,))):
    return lax.dot_general(a, b, (dims, ((), ())), preferred_element_type=jnp.float32)


def slot_loop(order_ref, begin, end, add):
    def step(block, carry):
        for offset in range(STEP):
            place = begin + block * STEP + offset
            add(order_ref[0, place], order_ref[1, place], order_ref[2, place], place < end)
        return carry

    lax.fori_loop(0, (end - begin + STEP - 1) // STEP, step, 0)


def forward_slots(stage, base, trash, order_ref, ends_ref, values_ref, panel_ref, acc_ref):
    def add(slot, tile, source, live):
        product = dot(values_ref[slot], panel_ref[source])
        acc_ref[jnp.where(live, base + tile, trash)] += product

    slot_loop(order_ref, ends_ref[stage], ends_ref[stage + 1], add)


def outer_kernel(order_ref, ends_ref, values_ref, panel_ref, *refs):
    next_ref, back_ref, up_ref, down_ref, acc_ref = refs
    acc_ref[...] = jnp.zeros_like(acc_ref)
    trash = 3 * FAR
    for stage in range(1, STAGES):
        base = (min(stage, 3) - 1) * FAR
        forward_slots(stage, base, trash, order_ref, ends_ref, values_ref, panel_ref, acc_ref)
    next_ref[...] = acc_ref[:FAR].astype(jnp.bfloat16)
    back_ref[...] = acc_ref[FAR : 2 * FAR].astype(jnp.bfloat16)
    up_ref[...] = acc_ref[2 * FAR : 2 * FAR + HALF].astype(jnp.bfloat16)
    down_ref[...] = acc_ref[2 * FAR + HALF : 3 * FAR].astype(jnp.bfloat16)


def forward_outer(order, ends, values, panel):
    whole = jax.ShapeDtypeStruct((FAR, TILE, FIN), jnp.bfloat16)
    half = jax.ShapeDtypeStruct((HALF, TILE, FIN), jnp.bfloat16)
    return pl.pallas_call(
        outer_kernel,
        out_shape=(whole, whole, half, half),
        in_specs=[SMEM, SMEM, VMEM, VMEM],
        out_specs=(VMEM,) * 4,
        scratch_shapes=[pltpu.VMEM((3 * FAR + 1, TILE, FIN), jnp.float32)],
        compiler_params=LIMIT,
    )(order, ends, values, panel)


def inner_kernel(order_ref, ends_ref, values_ref, panel_ref, acc_ref):
    acc_ref[...] = jnp.zeros_like(acc_ref)
    forward_slots(0, 0, FAR, order_ref, ends_ref, values_ref, panel_ref, acc_ref)


def forward_inner(order, ends, values, panel):
    return pl.pallas_call(
        inner_kernel,
        out_shape=jax.ShapeDtypeStruct((FAR + 1, TILE, FIN), jnp.float32),
        in_specs=[SMEM, SMEM, VMEM, VMEM],
        out_specs=VMEM,
        compiler_params=LIMIT,
    )(order, ends, values, panel)


def local_kernel(parts_ref, cot_ref, weight_ref, bias_ref, act_ref, proj_ref, grads_ref):
    agg = parts_ref[0].astype(jnp.float32)
    for i in range(1, FAR):
        agg = agg + parts_ref[i].astype(jnp.float32)
    upper = agg.astype(jnp.bfloat16)
    lower = (agg - upper.astype(jnp.float32)).astype(jnp.bfloat16)
    weight = weight_ref[...]
    preact = dot(upper, weight) + dot(lower, weight) + bias_ref[...]
    sigmoid = 1.0 / (1.0 + jnp.exp(-preact))
    act_ref[...] = (preact * sigmoid).astype(jnp.bfloat16)
    cot = cot_ref[...].astype(jnp.float32)
    grad = (cot * sigmoid * (1.0 + preact * (1.0 - sigmoid))).astype(jnp.bfloat16)
    proj_ref[...] = dot(weight, grad, ((1,), (1,))).astype(jnp.bfloat16)
    over_nodes = ((0,), (0,))
    wgrad = dot(upper, grad, over_nodes) + dot(lower, grad, over_nodes)
    bgrad = jnp.sum(grad.astype(jnp.float32), axis=0, keepdims=True)
    rows = FIN // 8
    for j in range(8):
        grads_ref[j, :rows, :] = wgrad[j * rows : (j + 1) * rows, :FIN]
        grads_ref[8 + j, :rows, :] = wgrad[j * rows : (j + 1) * rows, FIN:]
    tail = jnp.concatenate(
        [bgrad[:, :FIN], bgrad[:, FIN:], jnp.zeros((SHARE - rows - 2, FIN), jnp.float32)], axis=0
    )
    for j in range(CT):
        grads_ref[j, rows:, :] = tail


def local_part(parts, cot, weight, bias):
    return pl.pallas_call(
        local_kernel,
        out_shape=(
            jax.ShapeDtypeStruct((TILE, HID), jnp.bfloat16),
            jax.ShapeDtypeStruct((FIN, TILE), jnp.bfloat16),
            jax.ShapeDtypeStruct((CT, SHARE, FIN), jnp.float32),
        ),
        in_specs=[VMEM] * 4,
        out_specs=(VMEM, VMEM, VMEM),
        compiler_params=LIMIT,
    )(parts, cot, weight, bias)


def repeat_kernel(features_ref, out_ref):
    features = features_ref[...]
    for i in range(CT):
        out_ref[i] = features


def repeat(features):
    return pl.pallas_call(
        repeat_kernel,
        out_shape=jax.ShapeDtypeStruct((CT, TILE, FIN), jnp.bfloat16),
        in_specs=[VMEM],
        out_specs=VMEM,
        compiler_params=LIMIT,
    )(features)


def spread_kernel(proj_ref, grads_ref, out_ref):
    share = grads_ref[0]
    for i in range(1, CT):
        share = share + grads_ref[i]
    share = jnp.concatenate([share, jnp.zeros((EXTRA - SHARE, FIN), jnp.float32)], axis=0)
    share = share.astype(jnp.bfloat16)
    proj = proj_ref[...]
    for i in range(FAR):
        out_ref[i, :TILE, :] = proj
        out_ref[i, TILE:, :] = share


def spread(proj, grads):
    return pl.pallas_call(
        spread_kernel,
        out_shape=jax.ShapeDtypeStruct((FAR, TILE + EXTRA, TILE), jnp.bfloat16),
        in_specs=[VMEM, VMEM],
        out_specs=VMEM,
        compiler_params=LIMIT,
    )(proj, grads)


def join_kernel(parts_ref, out_ref, up_ref, down_ref):
    share = parts_ref[0, TILE:, :].astype(jnp.float32)
    for i in range(1, FAR):
        share = share + parts_ref[i, TILE:, :].astype(jnp.float32)
    share = share.astype(jnp.bfloat16)
    middle = HALF * TILE
    for i in range(HALF):
        low = parts_ref[i, :TILE, :]
        out_ref[i * TILE : (i + 1) * TILE, :] = low
        up_ref[i * TILE : (i + 1) * TILE, :] = low
        high = parts_ref[HALF + i, :TILE, :]
        begin = EXTRA + i * TILE
        out_ref[middle + begin : middle + begin + TILE, :] = high
        down_ref[begin : begin + TILE, :] = high
    out_ref[middle : middle + EXTRA, :] = share
    up_ref[middle:, :] = share
    down_ref[:EXTRA, :] = share


def join(parts):
    whole = jax.ShapeDtypeStruct((FAR * TILE + EXTRA, TILE), jnp.bfloat16)
    half = jax.ShapeDtypeStruct((HALF * TILE + EXTRA, TILE), jnp.bfloat16)
    return pl.pallas_call(
        join_kernel,
        out_shape=(whole, half, half),
        in_specs=[VMEM],
        out_specs=(VMEM,) * 3,
        compiler_params=LIMIT,
    )(parts)


def backward_slots(stage, order_ref, ends_ref, values_ref, panel_ref, acc_ref):
    def add(slot, tile, source, live):
        if stage == 4:
            begin = jnp.maximum(tile - HALF, 0) * TILE + EXTRA
        elif stage == 3:
            begin = jnp.minimum(tile, HALF - 1) * TILE
        else:
            begin = tile * TILE + jnp.where(tile < HALF, 0, EXTRA)
        begin = pl.multiple_of(begin, EXTRA)
        product = dot(panel_ref[pl.ds(begin, TILE), :], values_ref[slot])
        acc_ref[jnp.where(live, source, CT)] += product

    slot_loop(order_ref, ends_ref[stage], ends_ref[stage + 1], add)


def first_kernel(order_ref, ends_ref, values_ref, panel_ref, acc_ref):
    acc_ref[...] = jnp.zeros_like(acc_ref)
    backward_slots(0, order_ref, ends_ref, values_ref, panel_ref, acc_ref)


def last_kernel(order_ref, ends_ref, index_ref, values_ref, *refs):
    panels, old_ref, out_ref, acc_ref, shares_ref = refs[:STAGES], *refs[STAGES:]
    acc_ref[...] = old_ref[...]
    for stage in range(1, STAGES):
        backward_slots(stage, order_ref, ends_ref, values_ref, panels[stage], acc_ref)
    out_ref[:, :TILE, :] = acc_ref[:CT].astype(jnp.bfloat16)
    middle = HALF * TILE
    for place, stage in enumerate((0, 1, 3, 2)):
        shares_ref[place] = panels[stage][middle : middle + EXTRA, :].astype(jnp.float32)
    share = shares_ref[index_ref[0]]
    for i in range(1, NEAR):
        share = share + shares_ref[index_ref[i]]
    share = share.astype(jnp.bfloat16)
    for j in range(CT):
        out_ref[j, TILE:, :] = share


ACC = jax.ShapeDtypeStruct((CT + 1, TILE, TILE), jnp.float32)


def backward_first(order, ends, values, panel):
    return pl.pallas_call(
        first_kernel,
        out_shape=ACC,
        in_specs=[SMEM, SMEM, VMEM, VMEM],
        out_specs=VMEM,
        compiler_params=LIMIT,
    )(order, ends, values, panel)


def backward_last(order, ends, index, values, panels, old):
    return pl.pallas_call(
        last_kernel,
        out_shape=jax.ShapeDtypeStruct((CT, TILE + EXTRA, TILE), jnp.bfloat16),
        in_specs=[SMEM, SMEM, SMEM, VMEM] + [VMEM] * (STAGES + 1),
        out_specs=VMEM,
        scratch_shapes=[
            pltpu.VMEM((CT + 1, TILE, TILE), jnp.float32),
            pltpu.VMEM((NEAR, EXTRA, TILE), jnp.float32),
        ],
        compiler_params=LIMIT,
    )(order, ends, index, values, *panels, old)


def final_kernel(factor, parts_ref, feature_ref, wgrad_ref, bgrad_ref):
    total = parts_ref[0, :TILE, :].astype(jnp.float32)
    for i in range(1, CT):
        total = total + parts_ref[i, :TILE, :].astype(jnp.float32)
    feature_ref[...] = total.T.astype(jnp.bfloat16)
    rows = FIN // 8
    for j in range(8):
        left = parts_ref[j, TILE : TILE + rows, :].astype(jnp.float32) * factor
        right = parts_ref[8 + j, TILE : TILE + rows, :].astype(jnp.float32) * factor
        wgrad_ref[j * rows : (j + 1) * rows, :FIN] = left
        wgrad_ref[j * rows : (j + 1) * rows, FIN:] = right
    tail = parts_ref[0, TILE + rows :, :].astype(jnp.float32) * factor
    bgrad_ref[:, :FIN] = tail[0:1]
    bgrad_ref[:, FIN:] = tail[1:2]


def final_part(parts, factor):
    return pl.pallas_call(
        functools.partial(final_kernel, factor),
        out_shape=(
            jax.ShapeDtypeStruct((TILE, FIN), jnp.bfloat16),
            jax.ShapeDtypeStruct((FIN, HID), jnp.float32),
            jax.ShapeDtypeStruct((1, HID), jnp.float32),
        ),
        in_specs=[VMEM],
        out_specs=(VMEM, VMEM, VMEM),
        compiler_params=LIMIT,
    )(parts)


def slot_order(rows, cols, count, zone):
    away = jnp.remainder(rows - zone, NEAR)
    split = jnp.where(rows // NEAR < HALF, 3, 4)
    stage = jnp.where(away == 2, split, jnp.where(away == 3, 2, away))
    slots = jnp.arange(CAP, dtype=jnp.int32)
    stage = jnp.where(slots < count, stage, STAGES)
    key = stage * CAP + slots
    rank = jnp.sum((key[None, :] < key[:, None]).astype(jnp.int32), axis=1)
    places = jnp.arange(CAP + STEP, dtype=jnp.int32)
    chosen = (rank[None, :] == places[:, None]).astype(jnp.int32)
    lists = jnp.stack([slots, rows // NEAR, cols])
    order = jnp.sum(chosen[None] * lists[:, None, :], axis=2)
    ends = jnp.sum(
        (stage[None, :] < jnp.arange(STAGES + 1, dtype=jnp.int32)[:, None]).astype(jnp.int32), axis=1
    )
    return order, ends


def local(features, weight, out_bias, tile_values, tile_rows, band_offsets, tile_count, cotangent):
    values = tile_values[0, 0]
    rows = tile_rows[0, 0]
    cols = jnp.remainder(rows * CT // RT + band_offsets[0, 0], CT)
    zone = lax.axis_index("zb")
    order, ends = slot_order(rows, cols, tile_count[0, 0], zone)
    panel = lax.all_to_all(repeat(features), ROW, 0, 0, tiled=True)
    to_next, to_back, to_up, to_down = forward_outer(order, ends, values, panel)
    arrived = (shift(to_next, 1), shift(to_back, -1))
    arrived += (jnp.concatenate([shift(to_up, 2), shift(to_down, -2)], axis=0),)
    summed = forward_inner(order, ends, values, panel)[:FAR]
    for part in arrived:
        summed = summed + part.astype(jnp.float32)
    parts = lax.all_to_all(summed.astype(jnp.bfloat16), GROUP, 0, 0, tiled=True)
    activated, proj, grads = local_part(parts, cotangent, weight, out_bias.reshape(1, HID))
    grads = lax.all_to_all(grads, ROW, 0, 0, tiled=True)
    targets = lax.all_to_all(spread(proj, grads), GROUP, 0, 0, tiled=True)
    panel, up, down = join(targets)
    panels = [panel, shift(panel, -1), shift(panel, 1), shift(up, 2), shift(down, -2)]
    acc = backward_first(order, ends, values, panel)
    index = jnp.remainder(jnp.arange(NEAR, dtype=jnp.int32) - zone, NEAR)
    back = backward_last(order, ends, index, values, panels, acc)
    back = lax.all_to_all(back, ROW, 0, 0, tiled=True)
    nodes = TILE * lax.axis_size(ROW) * lax.axis_size(COL)
    feature_grad, weight_grad, bias_grad = final_part(back, 1.0 / math.sqrt(nodes))
    return (activated, feature_grad, weight_grad, bias_grad.reshape(HID))


def solution(mesh):
    axes = ROW + COL
    fine = Mesh(mesh.devices.reshape(2, 4, 2, 4, DEPTH // NEAR, NEAR), axes)
    placed = (
        P(COL + ROW, None),
        P(),
        P(),
        P(ROW, COL, None, None, None),
        P(ROW, COL, None),
        P(ROW, COL, None),
        P(ROW, COL),
        P(ROW + COL, None),
    )
    return jax.shard_map(
        local,
        mesh=fine,
        in_specs=placed,
        out_specs=(P(ROW + COL, None), P(COL + ROW, None), P(), P()),
        check_vma=False,
    )
```

time: 219 us -> 171 us (0.78)
  blocking collectives: 169 us -> 88.6 us
  starting transfers between devices: 22.3 us -> 44.7 us
  waiting for transfers between devices: 15.1 us -> 23.5 us
    all_to_all x3 -> x4, blocking collectives: 169 us -> 88.6 us  [the longest x1 28.5 us: local(): parts = lax.all_to_all(summed.astype(jnp.bfloat16), GROUP, 0, 0, tiled=True)]
    ppermute x0 -> x8, starting transfers between devices: none -> 30.8 us  [shift(): lax.ppermute(block, LINE, [(z, (z + steps) % DEPTH) for z in range(DEPTH)])]
    ppermute x0 -> x8, waiting for transfers between devices: none -> 16.1 us  [shift(): lax.ppermute(block, LINE, [(z, (z + steps) % DEPTH) for z in range(DEPTH)])]
    all_to_all x2 -> x1, starting transfers between devices: 22.3 us -> 13.9 us  [local(): panel = lax.all_to_all(repeat(features), ROW, 0, 0, tiled=True)]
    all_to_all x2 -> x1, waiting for transfers between devices: 15.1 us -> 7.35 us  [local(): panel = lax.all_to_all(repeat(features), ROW, 0, 0, tiled=True)]
    pallas_call x2 -> x7, Pallas kernels: 4.01 us -> 5.89 us  [the longest x1 1.6 us: forward_outer(): pl.pallas_call(outer_kernel, out_shape=(whole, whole, half, half), in_spe...]
  transfers between devices with their start and end apart: 2 -> 9, of which waited for: 2 -> 5; matrix products, arithmetic and copies ran while one was open for 0% -> 1% of each run, Pallas kernels for 0% -> 1%
where the time goes in v2:
time: 171 us; the launch traced here: 170 us
  blocking collectives  88.6 us (52%)
  starting transfers between devices  44.7 us (26%)
  waiting for transfers between devices  23.5 us (14%)
  Pallas kernels  7.53 us (4%)
  local copies, waits for them, and re-layouts  2.37 us (1%)
  other arithmetic  2.05 us (1%)
    ppermute x8, starting transfers between devices, shift(): lax.ppermute(block, LINE, [(z, (z + steps) % DEPTH) for z in range(DEPTH)])  30.8 us
    all_to_all x1, blocking collectives, local(): parts = lax.all_to_all(summed.astype(jnp.bfloat16), GROUP, 0, 0, tiled=True)  28.5 us
    all_to_all x1, blocking collectives, local(): targets = lax.all_to_all(spread(proj, grads), GROUP, 0, 0, tiled=True)  27.7 us
    all_to_all x1, blocking collectives, local(): back = lax.all_to_all(back, ROW, 0, 0, tiled=True)  16.7 us
    ppermute x8, waiting for transfers between devices, shift(): lax.ppermute(block, LINE, [(z, (z + steps) % DEPTH) for z in range(DEPTH)])  16.1 us
    all_to_all x1, blocking collectives, local(): grads = lax.all_to_all(grads, ROW, 0, 0, tiled=True)  15.7 us
    all_to_all x1, starting transfers between devices, local(): panel = lax.all_to_all(repeat(features), ROW, 0, 0, tiled=True)  13.9 us
    all_to_all x1, waiting for transfers between devices, local(): panel = lax.all_to_all(repeat(features), ROW, 0, 0, tiled=True)  7.35 us
  transfers between devices with their start and end apart: 9, of which 5 were waited for; matrix products, arithmetic and copies ran while one was open for 1% of the time, Pallas kernels for 1%

profile of v2, /device:TPU:1, one launch (start us, length us, event | category | flops | bytes accessed | tf_op | source)
XLA Modules:
  0.0 170.2 jit_solution(5422545470115942612)
XLA Ops:
  0.6 0.0 copy-start.4
  0.6 0.7 copy-done.4
  1.4 0.9 shard_map.111
  2.3 13.9 %all-to-all-start = ((bf16[16,128,128]{2,1,0:T(8,128)(2,1)}), bf16[16,128,128]{2,1,0:T(8,128)(2,1)S(1)}, u32[]{:S(2)}, u32[]{:S(2)}) async-start(bf16[16,128,128]{2,1,0:T(8,128)(2,1)} %shard_map.111), calls=%async_computation | async-start | bytes 1048576 | tf_op jit(solution)/shard_map/all_to_all | solution.py:330
  16.2 0.7 and_select_fusion.3
  17.5 0.7 iota_add_fusion
  18.2 0.1 convert_reduce_fusion.1.ends_ref
  18.3 0.2 convert_reduce_fusion
  18.5 0.1 fusion.3
  18.6 0.1 multiply_reduce_fusion.order_ref
  18.7 7.4 %all-to-all-done.panel_ref = bf16[16,128,128]{2,1,0:T(8,128)(2,1)S(1)} async-done(((bf16[16,128,128]{2,1,0:T(8,128)(2,1)}), bf16[16,128,128]{2,1,0:T(8,128)(2,1)S(1)}, u32[]{:S(2)}, u32[]{:S(2)}) %all-to-all-start) | async-done | bytes 524320 | tf_op jit(solution)/shard_map/all_to_all | solution.py:330
  26.0 1.6 copy-done
  27.6 1.6 shard_map.113
  29.2 1.9 %collective-permute-start = (bf16[12,128,128]{2,1,0:T(8,128)(2,1)S(1)}, bf16[12,128,128]{2,1,0:T(8,128)(2,1)S(1)}, u32[]{:S(2)}, u32[]{:S(2)}) collective-permute-start(bf16[12,128,128]{2,1,0:T(8,128)(2,1)S(1)} %get-tuple-element.17), channel_id=1, source_target_pairs={{0,1},{1,2},{2,3},{3,4},{4,5},{5,6},{6,7},{7,8},{8,9},{9,10},{10,1... | collective-permute-start | bytes 1179656 | tf_op jit(solution)/shard_map/ppermute | solution.py:36
  31.2 7.7 %collective-permute-start.1 = (bf16[12,128,128]{2,1,0:T(8,128)(2,1)S(1)}, bf16[12,128,128]{2,1,0:T(8,128)(2,1)S(1)}, u32[]{:S(2)}, u32[]{:S(2)}) collective-permute-start(bf16[12,128,128]{2,1,0:T(8,128)(2,1)S(1)} %get-tuple-element.18), channel_id=1, source_target_pairs={{0,11},{1,0},{2,1},{3,2},{4,3},{5,4},{6,5},{7,6},{8,7},{9,8},{10,9... | collective-permute-start | bytes 1179656 | tf_op jit(solution)/shard_map/ppermute | solution.py:36
  38.8 1.9 %collective-permute-start.2 = (bf16[6,128,128]{2,1,0:T(8,128)(2,1)S(1)}, bf16[6,128,128]{2,1,0:T(8,128)(2,1)S(1)}, u32[]{:S(2)}, u32[]{:S(2)}) collective-permute-start(bf16[6,128,128]{2,1,0:T(8,128)(2,1)S(1)} %get-tuple-element.19), channel_id=1, source_target_pairs={{0,2},{1,3},{2,4},{3,5},{4,6},{5,7},{6,8},{7,9},{8,10},{9,11},{10,... | collective-permute-start | bytes 589832 | tf_op jit(solution)/shard_map/ppermute | solution.py:36
  40.8 5.5 %collective-permute-start.3 = (bf16[6,128,128]{2,1,0:T(8,128)(2,1)S(1)}, bf16[6,128,128]{2,1,0:T(8,128)(2,1)S(1)}, u32[]{:S(2)}, u32[]{:S(2)}) collective-permute-start(bf16[6,128,128]{2,1,0:T(8,128)(2,1)S(1)} %get-tuple-element.20), channel_id=1, source_target_pairs={{0,10},{1,11},{2,0},{3,1},{4,2},{5,3},{6,4},{7,5},{8,6},{9,7},{10,... | collective-permute-start | bytes 589832 | tf_op jit(solution)/shard_map/ppermute | solution.py:36
  46.2 0.9 shard_map.112
  47.1 0.0 copy-start.2
  47.1 0.0 copy-start.3
  47.1 0.0 copy-start.5
  47.2 5.1 %collective-permute-done.2 = bf16[6,128,128]{2,1,0:T(8,128)(2,1)S(1)} collective-permute-done((bf16[6,128,128]{2,1,0:T(8,128)(2,1)S(1)}, bf16[6,128,128]{2,1,0:T(8,128)(2,1)S(1)}, u32[]{:S(2)}, u32[]{:S(2)}) %collective-permute-start.2) | collective-permute-done | bytes 196640 | tf_op jit(solution)/shard_map/ppermute | solution.py:36
  52.3 2.3 %collective-permute-done.3 = bf16[6,128,128]{2,1,0:T(8,128)(2,1)S(1)} collective-permute-done((bf16[6,128,128]{2,1,0:T(8,128)(2,1)S(1)}, bf16[6,128,128]{2,1,0:T(8,128)(2,1)S(1)}, u32[]{:S(2)}, u32[]{:S(2)}) %collective-permute-start.3) | collective-permute-done | bytes 196640 | tf_op jit(solution)/shard_map/ppermute | solution.py:36
  54.6 0.0 collective-permute-done
  54.6 0.0 collective-permute-done.1
  54.6 0.2 fusion.2
  54.8 0.0 copy-start.1
  54.8 28.5 %all_to_all.25.parts_ref = bf16[12,128,128]{2,1,0:T(8,128)(2,1)S(1)} all-to-all(bf16[12,128,128]{2,1,0:T(8,128)(2,1)S(1)} %fusion.2), channel_id=1, replica_groups=mesh['yl'=2,'x'=4,'core'=2,'yh'=4,'za'=3,'zb'=4] {'yh','za'}, dimensions={0} | all-to-all | bytes 786432 | tf_op jit(solution)/shard_map/all_to_all | solution.py:337
  83.3 0.0 copy-done.2
  83.3 0.0 copy-done.3
  83.3 0.0 copy-done.5
  83.3 0.9 shard_map.114
  84.2 15.7 %all_to_all.26.grads_ref = f32[16,24,128]{2,1,0:T(8,128)S(1)} all-to-all(f32[16,24,128]{2,1,0:T(8,128)S(1)} %get-tuple-element.23), channel_id=1, replica_groups=mesh['yl'=2,'x'=4,'core'=2,'yh'=4,'za'=3,'zb'=4] {'yl','x','core'}, dimensions={0} | all-to-all | bytes 393216 | tf_op jit(solution)/shard_map/all_to_all | solution.py:339
  100.0 0.1 shard_map.115
  100.0 27.7 %all_to_all.27.parts_ref = bf16[12,160,128]{2,1,0:T(8,128)(2,1)S(1)} all-to-all(bf16[12,160,128]{2,1,0:T(8,128)(2,1)S(1)} %shard_map.115), channel_id=1, replica_groups=mesh['yl'=2,'x'=4,'core'=2,'yh'=4,'za'=3,'zb'=4] {'yh','za'}, dimensions={0} | all-to-all | bytes 983040 | tf_op jit(solution)/shard_map/all_to_all | solution.py:340
  127.7 0.1 shard_map.116
  127.8 1.9 %collective-permute-start.5 = (bf16[1568,128]{1,0:T(8,128)(2,1)S(1)}, bf16[1568,128]{1,0:T(8,128)(2,1)S(1)}, u32[]{:S(2)}, u32[]{:S(2)}) collective-permute-start(bf16[1568,128]{1,0:T(8,128)(2,1)S(1)} %get-tuple-element.24.panel_ref.refs_0_), channel_id=1, source_target_pairs={{0,1},{1,2},{2,3},{3,4},{4,5},{5,6},{6,7},{7,8},{8,9},{9,10},{10,1... | collective-permute-start | bytes 1204232 | tf_op jit(solution)/shard_map/ppermute | solution.py:36
  129.8 4.6 %collective-permute-start.4 = (bf16[1568,128]{1,0:T(8,128)(2,1)S(1)}, bf16[1568,128]{1,0:T(8,128)(2,1)S(1)}, u32[]{:S(2)}, u32[]{:S(2)}) collective-permute-start(bf16[1568,128]{1,0:T(8,128)(2,1)S(1)} %get-tuple-element.24.panel_ref.refs_0_), channel_id=1, source_target_pairs={{0,11},{1,0},{2,1},{3,2},{4,3},{5,4},{6,5},{7,6},{8,7},{9,8},{10,9... | collective-permute-start | bytes 1204232 | tf_op jit(solution)/shard_map/ppermute | solution.py:36
  134.3 1.9 %collective-permute-start.6 = (bf16[800,128]{1,0:T(8,128)(2,1)S(1)}, bf16[800,128]{1,0:T(8,128)(2,1)S(1)}, u32[]{:S(2)}, u32[]{:S(2)}) collective-permute-start(bf16[800,128]{1,0:T(8,128)(2,1)S(1)} %get-tuple-element.25), channel_id=1, source_target_pairs={{0,2},{1,3},{2,4},{3,5},{4,6},{5,7},{6,8},{7,9},{8,10},{9,11},{10,... | collective-permute-start | bytes 614408 | tf_op jit(solution)/shard_map/ppermute | solution.py:36
  136.3 5.5 %collective-permute-start.7 = (bf16[800,128]{1,0:T(8,128)(2,1)S(1)}, bf16[800,128]{1,0:T(8,128)(2,1)S(1)}, u32[]{:S(2)}, u32[]{:S(2)}) collective-permute-start(bf16[800,128]{1,0:T(8,128)(2,1)S(1)} %get-tuple-element.26), channel_id=1, source_target_pairs={{0,10},{1,11},{2,0},{3,1},{4,2},{5,3},{6,4},{7,5},{8,6},{9,7},{10,... | collective-permute-start | bytes 614408 | tf_op jit(solution)/shard_map/ppermute | solution.py:36
  141.8 0.9 shard_map.117.refs_5_
  142.6 1.8 %collective-permute-done.6.refs_3_ = bf16[800,128]{1,0:T(8,128)(2,1)S(1)} collective-permute-done((bf16[800,128]{1,0:T(8,128)(2,1)S(1)}, bf16[800,128]{1,0:T(8,128)(2,1)S(1)}, u32[]{:S(2)}, u32[]{:S(2)}) %collective-permute-start.6) | collective-permute-done | bytes 204832 | tf_op jit(solution)/shard_map/ppermute | solution.py:36
  144.5 6.9 %collective-permute-done.7.refs_4_ = bf16[800,128]{1,0:T(8,128)(2,1)S(1)} collective-permute-done((bf16[800,128]{1,0:T(8,128)(2,1)S(1)}, bf16[800,128]{1,0:T(8,128)(2,1)S(1)}, u32[]{:S(2)}, u32[]{:S(2)}) %collective-permute-start.7) | collective-permute-done | bytes 204832 | tf_op jit(solution)/shard_map/ppermute | solution.py:36
  151.3 0.0 collective-permute-done.5.refs_2_
  151.3 0.0 collective-permute-done.4.refs_1_
  151.3 1.5 shard_map.118
  152.8 16.7 %all_to_all.28.parts_ref = bf16[16,160,128]{2,1,0:T(8,128)(2,1)S(1)} all-to-all(bf16[16,160,128]{2,1,0:T(8,128)(2,1)S(1)} %shard_map.118), channel_id=1, replica_groups=mesh['yl'=2,'x'=4,'core'=2,'yh'=4,'za'=3,'zb'=4] {'yl','x','core'}, dimensions={0} | all-to-all | bytes 1310720 | tf_op jit(solution)/shard_map/all_to_all | solution.py:346
  169.5 0.8 shard_map.119
  (5 shorter events, 0.0 us)
Async XLA Ops:
  0.6 0.8 copy-start.4
  2.3 23.8 %all-to-all-start = ((bf16[16,128,128]{2,1,0:T(8,128)(2,1)}), bf16[16,128,128]{2,1,0:T(8,128)(2,1)S(1)}, u32[]{:S(2)}, u32[]{:S(2)}) async-start(bf16[16,128,128]{2,1,0:T(8,128)(2,1)} %shard_map.111), calls=%async_computation | async-start | bytes 1048576 | tf_op jit(solution)/shard_map/all_to_all | solution.py:330
  26.0 1.6 copy-start
  29.2 25.3 %collective-permute-start = (bf16[12,128,128]{2,1,0:T(8,128)(2,1)S(1)}, bf16[12,128,128]{2,1,0:T(8,128)(2,1)S(1)}, u32[]{:S(2)}, u32[]{:S(2)}) collective-permute-start(bf16[12,128,128]{2,1,0:T(8,128)(2,1)S(1)} %get-tuple-element.17), channel_id=1, source_target_pairs={{0,1},{1,2},{2,3},{3,4},{4,5},{5,6},{6,7},{7,8},{8,9},{9,10},{10,1... | collective-permute-start | bytes 1179656 | tf_op jit(solution)/shard_map/ppermute | solution.py:36
  31.2 23.4 %collective-permute-start.1 = (bf16[12,128,128]{2,1,0:T(8,128)(2,1)S(1)}, bf16[12,128,128]{2,1,0:T(8,128)(2,1)S(1)}, u32[]{:S(2)}, u32[]{:S(2)}) collective-permute-start(bf16[12,128,128]{2,1,0:T(8,128)(2,1)S(1)} %get-tuple-element.18), channel_id=1, source_target_pairs={{0,11},{1,0},{2,1},{3,2},{4,3},{5,4},{6,5},{7,6},{8,7},{9,8},{10,9... | collective-permute-start | bytes 1179656 | tf_op jit(solution)/shard_map/ppermute | solution.py:36
  38.8 13.5 %collective-permute-start.2 = (bf16[6,128,128]{2,1,0:T(8,128)(2,1)S(1)}, bf16[6,128,128]{2,1,0:T(8,128)(2,1)S(1)}, u32[]{:S(2)}, u32[]{:S(2)}) collective-permute-start(bf16[6,128,128]{2,1,0:T(8,128)(2,1)S(1)} %get-tuple-element.19), channel_id=1, source_target_pairs={{0,2},{1,3},{2,4},{3,5},{4,6},{5,7},{6,8},{7,9},{8,10},{9,11},{10,... | collective-permute-start | bytes 589832 | tf_op jit(solution)/shard_map/ppermute | solution.py:36
  40.8 13.8 %collective-permute-start.3 = (bf16[6,128,128]{2,1,0:T(8,128)(2,1)S(1)}, bf16[6,128,128]{2,1,0:T(8,128)(2,1)S(1)}, u32[]{:S(2)}, u32[]{:S(2)}) collective-permute-start(bf16[6,128,128]{2,1,0:T(8,128)(2,1)S(1)} %get-tuple-element.20), channel_id=1, source_target_pairs={{0,10},{1,11},{2,0},{3,1},{4,2},{5,3},{6,4},{7,5},{8,6},{9,7},{10,... | collective-permute-start | bytes 589832 | tf_op jit(solution)/shard_map/ppermute | solution.py:36
  47.1 36.2 %copy-start.2 = (bf16[128,256]{1,0:T(8,128)(2,1)S(1)}, bf16[128,256]{1,0:T(8,128)(2,1)}, u32[]{:S(2)}) copy-start(bf16[128,256]{1,0:T(8,128)(2,1)} %cot_ref.1) | copy-start | bytes 196612
  47.1 36.2 %copy-start.3 = (bf16[128,256]{1,0:T(8,128)(2,1)S(1)}, bf16[128,256]{1,0:T(8,128)(2,1)}, u32[]{:S(2)}) copy-start(bf16[128,256]{1,0:T(8,128)(2,1)} %weight_ref.1) | copy-start | bytes 196612
  47.1 36.2 %copy-start.5 = (f32[256]{0:T(256)S(1)}, f32[256]{0:T(256)}, u32[]{:S(2)}) copy-start(f32[256]{0:T(256)} %param.10) | copy-start | bytes 3076
  54.8 87.0 %copy-start.1 = (bf16[1,1,64,128,128]{4,3,2,1,0:T(8,128)(2,1)S(1)}, bf16[1,1,64,128,128]{4,3,2,1,0:T(8,128)(2,1)}, u32[]{:S(2)}) copy-start(bf16[1,1,64,128,128]{4,3,2,1,0:T(8,128)(2,1)} %param.11) | copy-start | bytes 6291460
  127.8 23.5 %collective-permute-start.5 = (bf16[1568,128]{1,0:T(8,128)(2,1)S(1)}, bf16[1568,128]{1,0:T(8,128)(2,1)S(1)}, u32[]{:S(2)}, u32[]{:S(2)}) collective-permute-start(bf16[1568,128]{1,0:T(8,128)(2,1)S(1)} %get-tuple-element.24.panel_ref.refs_0_), channel_id=1, source_target_pairs={{0,1},{1,2},{2,3},{3,4},{4,5},{5,6},{6,7},{7,8},{8,9},{9,10},{10,1... | collective-permute-start | bytes 1204232 | tf_op jit(solution)/shard_map/ppermute | solution.py:36
  129.8 21.6 %collective-permute-start.4 = (bf16[1568,128]{1,0:T(8,128)(2,1)S(1)}, bf16[1568,128]{1,0:T(8,128)(2,1)S(1)}, u32[]{:S(2)}, u32[]{:S(2)}) collective-permute-start(bf16[1568,128]{1,0:T(8,128)(2,1)S(1)} %get-tuple-element.24.panel_ref.refs_0_), channel_id=1, source_target_pairs={{0,11},{1,0},{2,1},{3,2},{4,3},{5,4},{6,5},{7,6},{8,7},{9,8},{10,9... | collective-permute-start | bytes 1204232 | tf_op jit(solution)/shard_map/ppermute | solution.py:36
  134.3 10.1 %collective-permute-start.6 = (bf16[800,128]{1,0:T(8,128)(2,1)S(1)}, bf16[800,128]{1,0:T(8,128)(2,1)S(1)}, u32[]{:S(2)}, u32[]{:S(2)}) collective-permute-start(bf16[800,128]{1,0:T(8,128)(2,1)S(1)} %get-tuple-element.25), channel_id=1, source_target_pairs={{0,2},{1,3},{2,4},{3,5},{4,6},{5,7},{6,8},{7,9},{8,10},{9,11},{10,... | collective-permute-start | bytes 614408 | tf_op jit(solution)/shard_map/ppermute | solution.py:36
  136.3 15.1 %collective-permute-start.7 = (bf16[800,128]{1,0:T(8,128)(2,1)S(1)}, bf16[800,128]{1,0:T(8,128)(2,1)S(1)}, u32[]{:S(2)}, u32[]{:S(2)}) collective-permute-start(bf16[800,128]{1,0:T(8,128)(2,1)S(1)} %get-tuple-element.26), channel_id=1, source_target_pairs={{0,10},{1,11},{2,0},{3,1},{4,2},{5,3},{6,4},{7,5},{8,6},{9,7},{10,... | collective-permute-start | bytes 614408 | tf_op jit(solution)/shard_map/ppermute | solution.py:36

commit v3 on v2

--- a/solution.py
+++ b/solution.py
@@ -18,6 +18,7 @@
 STEP = 8
 EXTRA = 32
 SHARE = 24
+PART = FIN * HID // (CT * TILE)
 NEAR = 4
 FAR = RT // NEAR
 HALF = FAR // 2
@@ -156,6 +157,30 @@
     )(features)
 
 
+def fetch_kernel(values_ref, out_ref, sems):
+    part = CAP // STEP
+    copies = []
+    for i in range(STEP):
+        rows = pl.ds(i * part, part)
+        copies.append(pltpu.make_async_copy(values_ref.at[rows], out_ref.at[rows], sems.at[i]))
+    for copy in copies:
+        copy.start()
+    for copy in copies:
+        copy.wait()
+
+
+def fetch(values):
+    return pl.pallas_call(
+        fetch_kernel,
+        out_shape=jax.ShapeDtypeStruct(values.shape, values.dtype),
+        in_specs=[pl.BlockSpec(memory_space=pl.ANY)],
+        out_specs=VMEM,
+        scratch_shapes=[pltpu.SemaphoreType.DMA((STEP,))],
+        compiler_params=LIMIT,
+        cost_estimate=pl.CostEstimate(flops=0, bytes_accessed=1 << 22, transcendentals=0),
+    )(values)
+
+
 def spread_kernel(proj_ref, grads_ref, out_ref):
     share = grads_ref[0]
     for i in range(1, CT):
@@ -229,8 +254,8 @@
     backward_slots(0, order_ref, ends_ref, values_ref, panel_ref, acc_ref)
 
 
-def last_kernel(order_ref, ends_ref, index_ref, values_ref, *refs):
-    panels, old_ref, out_ref, acc_ref, shares_ref = refs[:STAGES], *refs[STAGES:]
+def last_kernel(factor, order_ref, ends_ref, index_ref, values_ref, *refs):
+    panels, old_ref, out_ref, bgrad_ref, acc_ref, shares_ref = refs[:STAGES], *refs[STAGES:]
     acc_ref[...] = old_ref[...]
     for stage in range(1, STAGES):
         backward_slots(stage, order_ref, ends_ref, values_ref, panels[stage], acc_ref)
@@ -241,7 +266,9 @@
     share = shares_ref[index_ref[0]]
     for i in range(1, NEAR):
         share = share + shares_ref[index_ref[i]]
-    share = share.astype(jnp.bfloat16)
+    bgrad_ref[:, :FIN] = share[PART : PART + 1] * factor
+    bgrad_ref[:, FIN:] = share[PART + 1 : PART + 2] * factor
+    share = share[:PART].astype(jnp.bfloat16)
     for j in range(CT):
         out_ref[j, TILE:, :] = share
 
@@ -259,12 +286,15 @@
     )(order, ends, values, panel)
 
 
-def backward_last(order, ends, index, values, panels, old):
-    return pl.pallas_call(
-        last_kernel,
-        out_shape=jax.ShapeDtypeStruct((CT, TILE + EXTRA, TILE), jnp.bfloat16),
+def backward_last(factor, order, ends, index, values, panels, old):
+    return pl.pallas_call(
+        functools.partial(last_kernel, factor),
+        out_shape=(
+            jax.ShapeDtypeStruct((CT, TILE + PART, TILE), jnp.bfloat16),
+            jax.ShapeDtypeStruct((1, HID), jnp.float32),
+        ),
         in_specs=[SMEM, SMEM, SMEM, VMEM] + [VMEM] * (STAGES + 1),
-        out_specs=VMEM,
+        out_specs=(VMEM, VMEM),
         scratch_shapes=[
             pltpu.VMEM((CT + 1, TILE, TILE), jnp.float32),
             pltpu.VMEM((NEAR, EXTRA, TILE), jnp.float32),
@@ -273,20 +303,17 @@
     )(order, ends, index, values, *panels, old)
 
 
-def final_kernel(factor, parts_ref, feature_ref, wgrad_ref, bgrad_ref):
+def final_kernel(factor, parts_ref, feature_ref, wgrad_ref):
     total = parts_ref[0, :TILE, :].astype(jnp.float32)
     for i in range(1, CT):
         total = total + parts_ref[i, :TILE, :].astype(jnp.float32)
     feature_ref[...] = total.T.astype(jnp.bfloat16)
-    rows = FIN // 8
-    for j in range(8):
-        left = parts_ref[j, TILE : TILE + rows, :].astype(jnp.float32) * factor
-        right = parts_ref[8 + j, TILE : TILE + rows, :].astype(jnp.float32) * factor
-        wgrad_ref[j * rows : (j + 1) * rows, :FIN] = left
-        wgrad_ref[j * rows : (j + 1) * rows, FIN:] = right
-    tail = parts_ref[0, TILE + rows :, :].astype(jnp.float32) * factor
-    bgrad_ref[:, :FIN] = tail[0:1]
-    bgrad_ref[:, FIN:] = tail[1:2]
+    half = CT // 2
+    for j in range(half):
+        left = parts_ref[j, TILE:, :].astype(jnp.float32) * factor
+        right = parts_ref[half + j, TILE:, :].astype(jnp.float32) * factor
+        wgrad_ref[j * PART : (j + 1) * PART, :FIN] = left
+        wgrad_ref[j * PART : (j + 1) * PART, FIN:] = right
 
 
 def final_part(parts, factor):
@@ -295,10 +322,9 @@
         out_shape=(
             jax.ShapeDtypeStruct((TILE, FIN), jnp.bfloat16),
             jax.ShapeDtypeStruct((FIN, HID), jnp.float32),
-            jax.ShapeDtypeStruct((1, HID), jnp.float32),
         ),
         in_specs=[VMEM],
-        out_specs=(VMEM, VMEM, VMEM),
+        out_specs=(VMEM, VMEM),
         compiler_params=LIMIT,
     )(parts)
 
@@ -322,7 +348,7 @@
 
 
 def local(features, weight, out_bias, tile_values, tile_rows, band_offsets, tile_count, cotangent):
-    values = tile_values[0, 0]
+    values = fetch(tile_values[0, 0])
     rows = tile_rows[0, 0]
     cols = jnp.remainder(rows * CT // RT + band_offsets[0, 0], CT)
     zone = lax.axis_index("zb")
@@ -342,10 +368,10 @@
     panels = [panel, shift(panel, -1), shift(panel, 1), shift(up, 2), shift(down, -2)]
     acc = backward_first(order, ends, values, panel)
     index = jnp.remainder(jnp.arange(NEAR, dtype=jnp.int32) - zone, NEAR)
-    back = backward_last(order, ends, index, values, panels, acc)
+    factor = 1.0 / math.sqrt(TILE * lax.axis_size(ROW) * lax.axis_size(COL))
+    back, bias_grad = backward_last(factor, order, ends, index, values, panels, acc)
     back = lax.all_to_all(back, ROW, 0, 0, tiled=True)
-    nodes = TILE * lax.axis_size(ROW) * lax.axis_size(COL)
-    feature_grad, weight_grad, bias_grad = final_part(back, 1.0 / math.sqrt(nodes))
+    feature_grad, weight_grad = final_part(back, factor)
     return (activated, feature_grad, weight_grad, bias_grad.reshape(HID))
 
 

time: 171 us -> 169 us (0.988)
  blocking collectives: 88.6 us -> 86.1 us
where the time goes in v3:
time: 169 us; the launch traced here: 168 us
  blocking collectives  86.1 us (51%)
  starting transfers between devices  44.5 us (26%)
  waiting for transfers between devices  22.4 us (13%)
  Pallas kernels  9.23 us (5%)
  local copies, waits for them, and re-layouts  2.75 us (2%)
    ppermute x8, starting transfers between devices, shift(): lax.ppermute(block, LINE, [(z, (z + steps) % DEPTH) for z in range(DEPTH)])  30.6 us
    all_to_all x1, blocking collectives, local(): targets = lax.all_to_all(spread(proj, grads), GROUP, 0, 0, tiled=True)  28.1 us
    all_to_all x1, blocking collectives, local(): parts = lax.all_to_all(summed.astype(jnp.bfloat16), GROUP, 0, 0, tiled=True)  27 us
    ppermute x8, waiting for transfers between devices, shift(): lax.ppermute(block, LINE, [(z, (z + steps) % DEPTH) for z in range(DEPTH)])  16.6 us
    all_to_all x1, blocking collectives, local(): back = lax.all_to_all(back, ROW, 0, 0, tiled=True)  15.6 us
    all_to_all x1, blocking collectives, local(): grads = lax.all_to_all(grads, ROW, 0, 0, tiled=True)  15.4 us
    all_to_all x1, starting transfers between devices, local(): panel = lax.all_to_all(repeat(features), ROW, 0, 0, tiled=True)  13.9 us
    all_to_all x1, waiting for transfers between devices, local(): panel = lax.all_to_all(repeat(features), ROW, 0, 0, tiled=True)  5.79 us
  transfers between devices with their start and end apart: 9, of which 5 were waited for; matrix products, arithmetic and copies ran while one was open for 1% of the time, Pallas kernels for 1%

profile of v3, /device:TPU:1, one launch (start us, length us, event | category | flops | bytes accessed | tf_op | source)
XLA Modules:
  0.0 167.9 jit_solution(1773111884197384629)
XLA Ops:
  0.6 0.0 copy-start.3
  0.6 0.7 copy-done.3
  1.4 0.9 shard_map.112
  2.3 13.9 %all-to-all-start = ((bf16[16,128,128]{2,1,0:T(8,128)(2,1)}), bf16[16,128,128]{2,1,0:T(8,128)(2,1)S(1)}, u32[]{:S(2)}, u32[]{:S(2)}) async-start(bf16[16,128,128]{2,1,0:T(8,128)(2,1)} %shard_map.112), calls=%async_computation | async-start | bytes 1048576 | tf_op jit(solution)/shard_map/all_to_all | solution.py:356
  16.2 0.7 and_select_fusion.3
  17.5 0.0 copy-start
  17.5 1.6 copy-done
  19.1 0.2 shard_map.111.values_ref
  19.4 0.4 copy-done.5
  19.8 0.1 convert_reduce_fusion.1.ends_ref
  19.9 0.2 convert_reduce_fusion
  20.1 0.1 fusion.3
  20.1 0.1 multiply_reduce_fusion.order_ref
  20.3 5.8 %all-to-all-done.panel_ref = bf16[16,128,128]{2,1,0:T(8,128)(2,1)S(1)} async-done(((bf16[16,128,128]{2,1,0:T(8,128)(2,1)}), bf16[16,128,128]{2,1,0:T(8,128)(2,1)S(1)}, u32[]{:S(2)}, u32[]{:S(2)}) %all-to-all-start) | async-done | bytes 524320 | tf_op jit(solution)/shard_map/all_to_all | solution.py:356
  26.0 2.0 %shard_map.114 = (bf16[12,128,128]{2,1,0:T(8,128)(2,1)S(1)}, bf16[12,128,128]{2,1,0:T(8,128)(2,1)S(1)}, bf16[6,128,128]{2,1,0:T(8,128)(2,1)S(1)}, bf16[6,128,128]{2,1,0:T(8,128)(2,1)S(1)}) custom-call(s32[3,72]{1,0:T(4,128)S(1)} %multiply_reduce_fusion.order_ref, s32[6]{0:T(128)S(1)} %convert_reduce_fusion.1.ends_ref, ...), custom_call_target="tpu_custom_call" | custom-call | tf_op jit(solution)/shard_map/pallas_call | solution.py:78
  28.1 1.9 %collective-permute-start = (bf16[12,128,128]{2,1,0:T(8,128)(2,1)S(1)}, bf16[12,128,128]{2,1,0:T(8,128)(2,1)S(1)}, u32[]{:S(2)}, u32[]{:S(2)}) collective-permute-start(bf16[12,128,128]{2,1,0:T(8,128)(2,1)S(1)} %get-tuple-element.18), channel_id=1, source_target_pairs={{0,1},{1,2},{2,3},{3,4},{4,5},{5,6},{6,7},{7,8},{8,9},{9,10},{10,1... | collective-permute-start | bytes 1179656 | tf_op jit(solution)/shard_map/ppermute | solution.py:37
  30.0 7.4 %collective-permute-start.1 = (bf16[12,128,128]{2,1,0:T(8,128)(2,1)S(1)}, bf16[12,128,128]{2,1,0:T(8,128)(2,1)S(1)}, u32[]{:S(2)}, u32[]{:S(2)}) collective-permute-start(bf16[12,128,128]{2,1,0:T(8,128)(2,1)S(1)} %get-tuple-element.19), channel_id=1, source_target_pairs={{0,11},{1,0},{2,1},{3,2},{4,3},{5,4},{6,5},{7,6},{8,7},{9,8},{10,9... | collective-permute-start | bytes 1179656 | tf_op jit(solution)/shard_map/ppermute | solution.py:37
  37.5 1.9 %collective-permute-start.2 = (bf16[6,128,128]{2,1,0:T(8,128)(2,1)S(1)}, bf16[6,128,128]{2,1,0:T(8,128)(2,1)S(1)}, u32[]{:S(2)}, u32[]{:S(2)}) collective-permute-start(bf16[6,128,128]{2,1,0:T(8,128)(2,1)S(1)} %get-tuple-element.20), channel_id=1, source_target_pairs={{0,2},{1,3},{2,4},{3,5},{4,6},{5,7},{6,8},{7,9},{8,10},{9,11},{10,... | collective-permute-start | bytes 589832 | tf_op jit(solution)/shard_map/ppermute | solution.py:37
  39.4 5.5 %collective-permute-start.3 = (bf16[6,128,128]{2,1,0:T(8,128)(2,1)S(1)}, bf16[6,128,128]{2,1,0:T(8,128)(2,1)S(1)}, u32[]{:S(2)}, u32[]{:S(2)}) collective-permute-start(bf16[6,128,128]{2,1,0:T(8,128)(2,1)S(1)} %get-tuple-element.21), channel_id=1, source_target_pairs={{0,10},{1,11},{2,0},{3,1},{4,2},{5,3},{6,4},{7,5},{8,6},{9,7},{10,... | collective-permute-start | bytes 589832 | tf_op jit(solution)/shard_map/ppermute | solution.py:37
  44.9 0.9 shard_map.113
  45.7 0.0 copy-start.1
  45.7 0.0 copy-start.2
  45.7 0.0 copy-start.4
  45.8 5.2 %collective-permute-done.2 = bf16[6,128,128]{2,1,0:T(8,128)(2,1)S(1)} collective-permute-done((bf16[6,128,128]{2,1,0:T(8,128)(2,1)S(1)}, bf16[6,128,128]{2,1,0:T(8,128)(2,1)S(1)}, u32[]{:S(2)}, u32[]{:S(2)}) %collective-permute-start.2) | collective-permute-done | bytes 196640 | tf_op jit(solution)/shard_map/ppermute | solution.py:37
  50.9 2.8 %collective-permute-done.3 = bf16[6,128,128]{2,1,0:T(8,128)(2,1)S(1)} collective-permute-done((bf16[6,128,128]{2,1,0:T(8,128)(2,1)S(1)}, bf16[6,128,128]{2,1,0:T(8,128)(2,1)S(1)}, u32[]{:S(2)}, u32[]{:S(2)}) %collective-permute-start.3) | collective-permute-done | bytes 196640 | tf_op jit(solution)/shard_map/ppermute | solution.py:37
  53.7 0.0 collective-permute-done
  53.7 0.0 collective-permute-done.1
  53.7 0.2 fusion.2
  53.9 27.0 %all_to_all.25.parts_ref = bf16[12,128,128]{2,1,0:T(8,128)(2,1)S(1)} all-to-all(bf16[12,128,128]{2,1,0:T(8,128)(2,1)S(1)} %fusion.2), channel_id=1, replica_groups=mesh['yl'=2,'x'=4,'core'=2,'yh'=4,'za'=3,'zb'=4] {'yh','za'}, dimensions={0} | all-to-all | bytes 786432 | tf_op jit(solution)/shard_map/all_to_all | solution.py:363
  81.0 0.0 copy-done.1
  81.0 0.0 copy-done.2
  81.0 0.9 shard_map.115
  81.9 15.4 %all_to_all.26.grads_ref = f32[16,24,128]{2,1,0:T(8,128)S(1)} all-to-all(f32[16,24,128]{2,1,0:T(8,128)S(1)} %get-tuple-element.24), channel_id=1, replica_groups=mesh['yl'=2,'x'=4,'core'=2,'yh'=4,'za'=3,'zb'=4] {'yl','x','core'}, dimensions={0} | all-to-all | bytes 393216 | tf_op jit(solution)/shard_map/all_to_all | solution.py:365
  97.3 0.1 shard_map.116
  97.3 28.1 %all_to_all.27.parts_ref = bf16[12,160,128]{2,1,0:T(8,128)(2,1)S(1)} all-to-all(bf16[12,160,128]{2,1,0:T(8,128)(2,1)S(1)} %shard_map.116), channel_id=1, replica_groups=mesh['yl'=2,'x'=4,'core'=2,'yh'=4,'za'=3,'zb'=4] {'yh','za'}, dimensions={0} | all-to-all | bytes 983040 | tf_op jit(solution)/shard_map/all_to_all | solution.py:366
  125.5 0.1 shard_map.117
  125.6 1.9 %collective-permute-start.5 = (bf16[1568,128]{1,0:T(8,128)(2,1)S(1)}, bf16[1568,128]{1,0:T(8,128)(2,1)S(1)}, u32[]{:S(2)}, u32[]{:S(2)}) collective-permute-start(bf16[1568,128]{1,0:T(8,128)(2,1)S(1)} %get-tuple-element.25.panel_ref.refs_0_), channel_id=1, source_target_pairs={{0,1},{1,2},{2,3},{3,4},{4,5},{5,6},{6,7},{7,8},{8,9},{9,10},{10,1... | collective-permute-start | bytes 1204232 | tf_op jit(solution)/shard_map/ppermute | solution.py:37
  127.5 4.6 %collective-permute-start.4 = (bf16[1568,128]{1,0:T(8,128)(2,1)S(1)}, bf16[1568,128]{1,0:T(8,128)(2,1)S(1)}, u32[]{:S(2)}, u32[]{:S(2)}) collective-permute-start(bf16[1568,128]{1,0:T(8,128)(2,1)S(1)} %get-tuple-element.25.panel_ref.refs_0_), channel_id=1, source_target_pairs={{0,11},{1,0},{2,1},{3,2},{4,3},{5,4},{6,5},{7,6},{8,7},{9,8},{10,9... | collective-permute-start | bytes 1204232 | tf_op jit(solution)/shard_map/ppermute | solution.py:37
  132.1 1.9 %collective-permute-start.6 = (bf16[800,128]{1,0:T(8,128)(2,1)S(1)}, bf16[800,128]{1,0:T(8,128)(2,1)S(1)}, u32[]{:S(2)}, u32[]{:S(2)}) collective-permute-start(bf16[800,128]{1,0:T(8,128)(2,1)S(1)} %get-tuple-element.26), channel_id=1, source_target_pairs={{0,2},{1,3},{2,4},{3,5},{4,6},{5,7},{6,8},{7,9},{8,10},{9,11},{10,... | collective-permute-start | bytes 614408 | tf_op jit(solution)/shard_map/ppermute | solution.py:37
  134.0 5.5 %collective-permute-start.7 = (bf16[800,128]{1,0:T(8,128)(2,1)S(1)}, bf16[800,128]{1,0:T(8,128)(2,1)S(1)}, u32[]{:S(2)}, u32[]{:S(2)}) collective-permute-start(bf16[800,128]{1,0:T(8,128)(2,1)S(1)} %get-tuple-element.27), channel_id=1, source_target_pairs={{0,10},{1,11},{2,0},{3,1},{4,2},{5,3},{6,4},{7,5},{8,6},{9,7},{10,... | collective-permute-start | bytes 614408 | tf_op jit(solution)/shard_map/ppermute | solution.py:37
  139.5 0.9 shard_map.118.refs_5_
  140.4 1.4 collective-permute-done.6.refs_3_
  141.8 7.3 %collective-permute-done.7.refs_4_ = bf16[800,128]{1,0:T(8,128)(2,1)S(1)} collective-permute-done((bf16[800,128]{1,0:T(8,128)(2,1)S(1)}, bf16[800,128]{1,0:T(8,128)(2,1)S(1)}, u32[]{:S(2)}, u32[]{:S(2)}) %collective-permute-start.7) | collective-permute-done | bytes 204832 | tf_op jit(solution)/shard_map/ppermute | solution.py:37
  149.1 0.0 collective-permute-done.5.refs_2_
  149.1 0.0 collective-permute-done.4.refs_1_
  149.1 2.5 %shard_map.119 = (bf16[16,144,128]{2,1,0:T(8,128)(2,1)S(1)}, f32[1,256]{1,0:T(1,128)}) custom-call(s32[3,72]{1,0:T(4,128)S(1)} %multiply_reduce_fusion.order_ref, s32[6]{0:T(128)S(1)} %convert_reduce_fusion.1.ends_ref, s32[4]{0:T(128)S(1)} %and_select_fusion.index_ref, bf16[64,128,128]{2,1,0:T(8,128)(2,1)S(1)} %shard_map.111.values_ref, ...), custom_call_target="tpu_custom_call" | custom-call | tf_op jit(solution)/shard_map/pallas_call | solution.py:290
  151.6 15.6 %all_to_all.28.parts_ref = bf16[16,144,128]{2,1,0:T(8,128)(2,1)S(1)} all-to-all(bf16[16,144,128]{2,1,0:T(8,128)(2,1)S(1)} %get-tuple-element.28), channel_id=1, replica_groups=mesh['yl'=2,'x'=4,'core'=2,'yh'=4,'za'=3,'zb'=4] {'yl','x','core'}, dimensions={0} | all-to-all | bytes 1179648 | tf_op jit(solution)/shard_map/all_to_all | solution.py:373
  167.1 0.8 shard_map.120
  (6 shorter events, 0.0 us)
Async XLA Ops:
  0.6 0.8 copy-start.3
  2.3 23.8 %all-to-all-start = ((bf16[16,128,128]{2,1,0:T(8,128)(2,1)}), bf16[16,128,128]{2,1,0:T(8,128)(2,1)S(1)}, u32[]{:S(2)}, u32[]{:S(2)}) async-start(bf16[16,128,128]{2,1,0:T(8,128)(2,1)} %shard_map.112), calls=%async_computation | async-start | bytes 1048576 | tf_op jit(solution)/shard_map/all_to_all | solution.py:356
  17.5 1.6 copy-start
  19.1 0.7 copy-start.5
  28.1 25.6 %collective-permute-start = (bf16[12,128,128]{2,1,0:T(8,128)(2,1)S(1)}, bf16[12,128,128]{2,1,0:T(8,128)(2,1)S(1)}, u32[]{:S(2)}, u32[]{:S(2)}) collective-permute-start(bf16[12,128,128]{2,1,0:T(8,128)(2,1)S(1)} %get-tuple-element.18), channel_id=1, source_target_pairs={{0,1},{1,2},{2,3},{3,4},{4,5},{5,6},{6,7},{7,8},{8,9},{9,10},{10,1... | collective-permute-start | bytes 1179656 | tf_op jit(solution)/shard_map/ppermute | solution.py:37
  30.0 23.7 %collective-permute-start.1 = (bf16[12,128,128]{2,1,0:T(8,128)(2,1)S(1)}, bf16[12,128,128]{2,1,0:T(8,128)(2,1)S(1)}, u32[]{:S(2)}, u32[]{:S(2)}) collective-permute-start(bf16[12,128,128]{2,1,0:T(8,128)(2,1)S(1)} %get-tuple-element.19), channel_id=1, source_target_pairs={{0,11},{1,0},{2,1},{3,2},{4,3},{5,4},{6,5},{7,6},{8,7},{9,8},{10,9... | collective-permute-start | bytes 1179656 | tf_op jit(solution)/shard_map/ppermute | solution.py:37
  37.5 13.5 %collective-permute-start.2 = (bf16[6,128,128]{2,1,0:T(8,128)(2,1)S(1)}, bf16[6,128,128]{2,1,0:T(8,128)(2,1)S(1)}, u32[]{:S(2)}, u32[]{:S(2)}) collective-permute-start(bf16[6,128,128]{2,1,0:T(8,128)(2,1)S(1)} %get-tuple-element.20), channel_id=1, source_target_pairs={{0,2},{1,3},{2,4},{3,5},{4,6},{5,7},{6,8},{7,9},{8,10},{9,11},{10,... | collective-permute-start | bytes 589832 | tf_op jit(solution)/shard_map/ppermute | solution.py:37
  39.4 14.3 %collective-permute-start.3 = (bf16[6,128,128]{2,1,0:T(8,128)(2,1)S(1)}, bf16[6,128,128]{2,1,0:T(8,128)(2,1)S(1)}, u32[]{:S(2)}, u32[]{:S(2)}) collective-permute-start(bf16[6,128,128]{2,1,0:T(8,128)(2,1)S(1)} %get-tuple-element.21), channel_id=1, source_target_pairs={{0,10},{1,11},{2,0},{3,1},{4,2},{5,3},{6,4},{7,5},{8,6},{9,7},{10,... | collective-permute-start | bytes 589832 | tf_op jit(solution)/shard_map/ppermute | solution.py:37
  45.7 35.2 %copy-start.1 = (bf16[128,256]{1,0:T(8,128)(2,1)S(1)}, bf16[128,256]{1,0:T(8,128)(2,1)}, u32[]{:S(2)}) copy-start(bf16[128,256]{1,0:T(8,128)(2,1)} %cot_ref.1) | copy-start | bytes 196612
  45.7 35.2 %copy-start.2 = (bf16[128,256]{1,0:T(8,128)(2,1)S(1)}, bf16[128,256]{1,0:T(8,128)(2,1)}, u32[]{:S(2)}) copy-start(bf16[128,256]{1,0:T(8,128)(2,1)} %weight_ref.1) | copy-start | bytes 196612
  45.7 35.2 %copy-start.4 = (f32[256]{0:T(256)S(1)}, f32[256]{0:T(256)}, u32[]{:S(2)}) copy-start(f32[256]{0:T(256)} %param.10) | copy-start | bytes 3076
  125.6 23.5 %collective-permute-start.5 = (bf16[1568,128]{1,0:T(8,128)(2,1)S(1)}, bf16[1568,128]{1,0:T(8,128)(2,1)S(1)}, u32[]{:S(2)}, u32[]{:S(2)}) collective-permute-start(bf16[1568,128]{1,0:T(8,128)(2,1)S(1)} %get-tuple-element.25.panel_ref.refs_0_), channel_id=1, source_target_pairs={{0,1},{1,2},{2,3},{3,4},{4,5},{5,6},{6,7},{7,8},{8,9},{9,10},{10,1... | collective-permute-start | bytes 1204232 | tf_op jit(solution)/shard_map/ppermute | solution.py:37
  127.5 21.6 %collective-permute-start.4 = (bf16[1568,128]{1,0:T(8,128)(2,1)S(1)}, bf16[1568,128]{1,0:T(8,128)(2,1)S(1)}, u32[]{:S(2)}, u32[]{:S(2)}) collective-permute-start(bf16[1568,128]{1,0:T(8,128)(2,1)S(1)} %get-tuple-element.25.panel_ref.refs_0_), channel_id=1, source_target_pairs={{0,11},{1,0},{2,1},{3,2},{4,3},{5,4},{6,5},{7,6},{8,7},{9,8},{10,9... | collective-permute-start | bytes 1204232 | tf_op jit(solution)/shard_map/ppermute | solution.py:37
  132.1 9.7 %collective-permute-start.6 = (bf16[800,128]{1,0:T(8,128)(2,1)S(1)}, bf16[800,128]{1,0:T(8,128)(2,1)S(1)}, u32[]{:S(2)}, u32[]{:S(2)}) collective-permute-start(bf16[800,128]{1,0:T(8,128)(2,1)S(1)} %get-tuple-element.26), channel_id=1, source_target_pairs={{0,2},{1,3},{2,4},{3,5},{4,6},{5,7},{6,8},{7,9},{8,10},{9,11},{10,... | collective-permute-start | bytes 614408 | tf_op jit(solution)/shard_map/ppermute | solution.py:37
  134.0 15.0 %collective-permute-start.7 = (bf16[800,128]{1,0:T(8,128)(2,1)S(1)}, bf16[800,128]{1,0:T(8,128)(2,1)S(1)}, u32[]{:S(2)}, u32[]{:S(2)}) collective-permute-start(bf16[800,128]{1,0:T(8,128)(2,1)S(1)} %get-tuple-element.27), channel_id=1, source_target_pairs={{0,10},{1,11},{2,0},{3,1},{4,2},{5,3},{6,4},{7,5},{8,6},{9,7},{10,... | collective-permute-start | bytes 614408 | tf_op jit(solution)/shard_map/ppermute | solution.py:37

commit v4 on v3

--- a/solution.py
+++ b/solution.py
@@ -19,15 +19,15 @@
 EXTRA = 32
 SHARE = 24
 PART = FIN * HID // (CT * TILE)
-NEAR = 4
+NEAR = 3
 FAR = RT // NEAR
-HALF = FAR // 2
 DEPTH = 12
-STAGES = 5
+STAGES = NEAR
 
 ROW = ("yl", "x", "core")
 COL = ("yh", "za", "zb")
-GROUP = ("yh", "za")
+TALL = 4
+WIDE = FAR // TALL
 LINE = ("za", "zb")
 
 SMEM = pl.BlockSpec(memory_space=pltpu.SMEM)
@@ -60,27 +60,23 @@
 
 
 def outer_kernel(order_ref, ends_ref, values_ref, panel_ref, *refs):
-    next_ref, back_ref, up_ref, down_ref, acc_ref = refs
+    outs, acc_ref = refs[:-1], refs[-1]
     acc_ref[...] = jnp.zeros_like(acc_ref)
-    trash = 3 * FAR
-    for stage in range(1, STAGES):
-        base = (min(stage, 3) - 1) * FAR
+    trash = (NEAR - 1) * FAR
+    for stage in range(1, NEAR):
+        base = (stage - 1) * FAR
         forward_slots(stage, base, trash, order_ref, ends_ref, values_ref, panel_ref, acc_ref)
-    next_ref[...] = acc_ref[:FAR].astype(jnp.bfloat16)
-    back_ref[...] = acc_ref[FAR : 2 * FAR].astype(jnp.bfloat16)
-    up_ref[...] = acc_ref[2 * FAR : 2 * FAR + HALF].astype(jnp.bfloat16)
-    down_ref[...] = acc_ref[2 * FAR + HALF : 3 * FAR].astype(jnp.bfloat16)
+        outs[stage - 1][...] = acc_ref[base : base + FAR].astype(jnp.bfloat16)
 
 
 def forward_outer(order, ends, values, panel):
-    whole = jax.ShapeDtypeStruct((FAR, TILE, FIN), jnp.bfloat16)
-    half = jax.ShapeDtypeStruct((HALF, TILE, FIN), jnp.bfloat16)
+    sent = jax.ShapeDtypeStruct((FAR, TILE, FIN), jnp.bfloat16)
     return pl.pallas_call(
         outer_kernel,
-        out_shape=(whole, whole, half, half),
+        out_shape=(sent,) * (NEAR - 1),
         in_specs=[SMEM, SMEM, VMEM, VMEM],
-        out_specs=(VMEM,) * 4,
-        scratch_shapes=[pltpu.VMEM((3 * FAR + 1, TILE, FIN), jnp.float32)],
+        out_specs=(VMEM,) * (NEAR - 1),
+        scratch_shapes=[pltpu.VMEM(((NEAR - 1) * FAR + 1, TILE, FIN), jnp.float32)],
         compiler_params=LIMIT,
     )(order, ends, values, panel)
 
@@ -188,7 +184,7 @@
     share = jnp.concatenate([share, jnp.zeros((EXTRA - SHARE, FIN), jnp.float32)], axis=0)
     share = share.astype(jnp.bfloat16)
     proj = proj_ref[...]
-    for i in range(FAR):
+    for i in range(WIDE):
         out_ref[i, :TILE, :] = proj
         out_ref[i, TILE:, :] = share
 
@@ -196,53 +192,59 @@
 def spread(proj, grads):
     return pl.pallas_call(
         spread_kernel,
-        out_shape=jax.ShapeDtypeStruct((FAR, TILE + EXTRA, TILE), jnp.bfloat16),
+        out_shape=jax.ShapeDtypeStruct((WIDE, TILE + EXTRA, TILE), jnp.bfloat16),
         in_specs=[VMEM, VMEM],
         out_specs=VMEM,
         compiler_params=LIMIT,
     )(proj, grads)
 
 
-def join_kernel(parts_ref, out_ref, up_ref, down_ref):
+def widen_kernel(parts_ref, out_ref):
     share = parts_ref[0, TILE:, :].astype(jnp.float32)
-    for i in range(1, FAR):
+    for i in range(1, WIDE):
         share = share + parts_ref[i, TILE:, :].astype(jnp.float32)
     share = share.astype(jnp.bfloat16)
-    middle = HALF * TILE
-    for i in range(HALF):
-        low = parts_ref[i, :TILE, :]
-        out_ref[i * TILE : (i + 1) * TILE, :] = low
-        up_ref[i * TILE : (i + 1) * TILE, :] = low
-        high = parts_ref[HALF + i, :TILE, :]
-        begin = EXTRA + i * TILE
-        out_ref[middle + begin : middle + begin + TILE, :] = high
-        down_ref[begin : begin + TILE, :] = high
-    out_ref[middle : middle + EXTRA, :] = share
-    up_ref[middle:, :] = share
-    down_ref[:EXTRA, :] = share
+    for i in range(WIDE):
+        tile = parts_ref[i, :TILE, :]
+        for j in range(TALL):
+            out_ref[j, i * TILE : (i + 1) * TILE, :] = tile
+    for j in range(TALL):
+        out_ref[j, WIDE * TILE :, :] = share
+
+
+def widen(parts):
+    return pl.pallas_call(
+        widen_kernel,
+        out_shape=jax.ShapeDtypeStruct((TALL, WIDE * TILE + EXTRA, TILE), jnp.bfloat16),
+        in_specs=[VMEM],
+        out_specs=VMEM,
+        compiler_params=LIMIT,
+    )(parts)
+
+
+def join_kernel(parts_ref, out_ref):
+    last = WIDE * TILE
+    share = parts_ref[0, last:, :].astype(jnp.float32)
+    for i in range(1, TALL):
+        share = share + parts_ref[i, last:, :].astype(jnp.float32)
+    for i in range(TALL):
+        out_ref[i * last : (i + 1) * last, :] = parts_ref[i, :last, :]
+    out_ref[FAR * TILE :, :] = share.astype(jnp.bfloat16)
 
 
 def join(parts):
-    whole = jax.ShapeDtypeStruct((FAR * TILE + EXTRA, TILE), jnp.bfloat16)
-    half = jax.ShapeDtypeStruct((HALF * TILE + EXTRA, TILE), jnp.bfloat16)
     return pl.pallas_call(
         join_kernel,
-        out_shape=(whole, half, half),
+        out_shape=jax.ShapeDtypeStruct((FAR * TILE + EXTRA, TILE), jnp.bfloat16),
         in_specs=[VMEM],
-        out_specs=(VMEM,) * 3,
+        out_specs=VMEM,
         compiler_params=LIMIT,
     )(parts)
 
 
 def backward_slots(stage, order_ref, ends_ref, values_ref, panel_ref, acc_ref):
     def add(slot, tile, source, live):
-        if stage == 4:
-            begin = jnp.maximum(tile - HALF, 0) * TILE + EXTRA
-        elif stage == 3:
-            begin = jnp.minimum(tile, HALF - 1) * TILE
-        else:
-            begin = tile * TILE + jnp.where(tile < HALF, 0, EXTRA)
-        begin = pl.multiple_of(begin, EXTRA)
+        begin = pl.multiple_of(tile * TILE, TILE)
         product = dot(panel_ref[pl.ds(begin, TILE), :], values_ref[slot])
         acc_ref[jnp.where(live, source, CT)] += product
 
@@ -260,9 +262,8 @@
     for stage in range(1, STAGES):
         backward_slots(stage, order_ref, ends_ref, values_ref, panels[stage], acc_ref)
     out_ref[:, :TILE, :] = acc_ref[:CT].astype(jnp.bfloat16)
-    middle = HALF * TILE
-    for place, stage in enumerate((0, 1, 3, 2)):
-        shares_ref[place] = panels[stage][middle : middle + EXTRA, :].astype(jnp.float32)
+    for stage in range(NEAR):
+        shares_ref[stage] = panels[stage][FAR * TILE :, :].astype(jnp.float32)
     share = shares_ref[index_ref[0]]
     for i in range(1, NEAR):
         share = share + shares_ref[index_ref[i]]
@@ -330,9 +331,7 @@
 
 
 def slot_order(rows, cols, count, zone):
-    away = jnp.remainder(rows - zone, NEAR)
-    split = jnp.where(rows // NEAR < HALF, 3, 4)
-    stage = jnp.where(away == 2, split, jnp.where(away == 3, 2, away))
+    stage = jnp.remainder(rows - zone, NEAR)
     slots = jnp.arange(CAP, dtype=jnp.int32)
     stage = jnp.where(slots < count, stage, STAGES)
     key = stage * CAP + slots
@@ -354,18 +353,18 @@
     zone = lax.axis_index("zb")
     order, ends = slot_order(rows, cols, tile_count[0, 0], zone)
     panel = lax.all_to_all(repeat(features), ROW, 0, 0, tiled=True)
-    to_next, to_back, to_up, to_down = forward_outer(order, ends, values, panel)
+    to_next, to_back = forward_outer(order, ends, values, panel)
     arrived = (shift(to_next, 1), shift(to_back, -1))
-    arrived += (jnp.concatenate([shift(to_up, 2), shift(to_down, -2)], axis=0),)
     summed = forward_inner(order, ends, values, panel)[:FAR]
     for part in arrived:
         summed = summed + part.astype(jnp.float32)
-    parts = lax.all_to_all(summed.astype(jnp.bfloat16), GROUP, 0, 0, tiled=True)
+    parts = lax.all_to_all(summed.astype(jnp.bfloat16), ("yh", "za"), 0, 0, tiled=True)
     activated, proj, grads = local_part(parts, cotangent, weight, out_bias.reshape(1, HID))
     grads = lax.all_to_all(grads, ROW, 0, 0, tiled=True)
-    targets = lax.all_to_all(spread(proj, grads), GROUP, 0, 0, tiled=True)
-    panel, up, down = join(targets)
-    panels = [panel, shift(panel, -1), shift(panel, 1), shift(up, 2), shift(down, -2)]
+    targets = lax.all_to_all(spread(proj, grads), "za", 0, 0, tiled=True)
+    targets = lax.all_to_all(widen(targets), "yh", 0, 0, tiled=True)
+    panel = join(targets)
+    panels = [panel, shift(panel, -1), shift(panel, 1)]
     acc = backward_first(order, ends, values, panel)
     index = jnp.remainder(jnp.arange(NEAR, dtype=jnp.int32) - zone, NEAR)
     factor = 1.0 / math.sqrt(TILE * lax.axis_size(ROW) * lax.axis_size(COL))

time: 169 us -> 171 us (1.012)
  blocking collectives: 86.1 us -> 101 us
  starting transfers between devices: 44.5 us -> 33.1 us
    ppermute x8 -> x4, starting transfers between devices: 30.6 us -> 19.2 us  [shift(): lax.ppermute(block, LINE, [(z, (z + steps) % DEPTH) for z in range(DEPTH)])]
    all_to_all x1, blocking collectives: 15.6 us -> 24.7 us  [local(): back = lax.all_to_all(back, ROW, 0, 0, tiled=True)]
    all_to_all x1, blocking collectives: 15.4 us -> 20.6 us  [local(): grads = lax.all_to_all(grads, ROW, 0, 0, tiled=True)]
    all_to_all x2 -> x3, blocking collectives: 55.2 us -> 55.9 us  [the longest x1 27.9 us: local(): lax.all_to_all(summed.astype(jnp.bfloat16), ('yh', 'za'), 0, 0, tiled=True)]
    ppermute x8 -> x4, waiting for transfers between devices: 16.6 us -> 16.6 us  [shift(): lax.ppermute(block, LINE, [(z, (z + steps) % DEPTH) for z in range(DEPTH)])]
  transfers between devices with their start and end apart: 9 -> 5, of which waited for: 5 -> 5; matrix products, arithmetic and copies ran while one was open for 1% -> 0% of each run, Pallas kernels for 1% -> 1%
where the time goes in v4:
time: 171 us; the launch traced here: 170 us
  blocking collectives  101 us (59%)
  starting transfers between devices  33.1 us (19%)
  waiting for transfers between devices  23.4 us (14%)
  Pallas kernels  7.75 us (5%)
  local copies, waits for them, and re-layouts  2.37 us (1%)
    all_to_all x1, blocking collectives, local(): lax.all_to_all(summed.astype(jnp.bfloat16), ('yh', 'za'), 0, 0, tiled=True)  27.9 us
    all_to_all x1, blocking collectives, local(): back = lax.all_to_all(back, ROW, 0, 0, tiled=True)  24.7 us
    all_to_all x1, blocking collectives, local(): grads = lax.all_to_all(grads, ROW, 0, 0, tiled=True)  20.6 us
    ppermute x4, starting transfers between devices, shift(): lax.ppermute(block, LINE, [(z, (z + steps) % DEPTH) for z in range(DEPTH)])  19.2 us
    ppermute x4, waiting for transfers between devices, shift(): lax.ppermute(block, LINE, [(z, (z + steps) % DEPTH) for z in range(DEPTH)])  16.6 us
    all_to_all x1, blocking collectives, local(): targets = lax.all_to_all(widen(targets), 'yh', 0, 0, tiled=True)  15.9 us
    all_to_all x1, starting transfers between devices, local(): panel = lax.all_to_all(repeat(features), ROW, 0, 0, tiled=True)  13.9 us
    all_to_all x1, blocking collectives, local(): targets = lax.all_to_all(spread(proj, grads), 'za', 0, 0, tiled=True)  12.2 us
  transfers between devices with their start and end apart: 5, of which 5 were waited for; matrix products, arithmetic and copies ran while one was open for 0% of the time, Pallas kernels for 1%

profile of v4, /device:TPU:1, one launch (start us, length us, event | category | flops | bytes accessed | tf_op | source)
XLA Modules:
  0.0 169.9 jit_solution(9770776595303570618)
XLA Ops:
  0.6 0.0 copy-start.3
  0.6 0.7 copy-done.3
  1.4 0.0 copy-start.5
  1.4 0.0 copy-start.6
  1.4 0.9 shard_map.112
  2.3 13.9 %all-to-all-start = ((bf16[16,128,128]{2,1,0:T(8,128)(2,1)}), bf16[16,128,128]{2,1,0:T(8,128)(2,1)S(1)}, u32[]{:S(2)}, u32[]{:S(2)}) async-start(bf16[16,128,128]{2,1,0:T(8,128)(2,1)} %shard_map.112), calls=%async_computation | async-start | bytes 1048576 | tf_op jit(solution)/shard_map/all_to_all | solution.py:355
  16.2 0.0 copy-done.5
  16.2 0.0 copy-done.6
  16.9 0.0 copy-start
  16.9 1.6 copy-done
  18.5 0.2 shard_map.111.values_ref
  18.7 0.1 convert_reduce_fusion.1.ends_ref
  18.9 0.2 convert_reduce_fusion
  19.0 0.1 fusion.2
  19.1 0.1 multiply_reduce_fusion.order_ref
  19.2 6.8 %all-to-all-done.panel_ref = bf16[16,128,128]{2,1,0:T(8,128)(2,1)S(1)} async-done(((bf16[16,128,128]{2,1,0:T(8,128)(2,1)}), bf16[16,128,128]{2,1,0:T(8,128)(2,1)S(1)}, u32[]{:S(2)}, u32[]{:S(2)}) %all-to-all-start) | async-done | bytes 524320 | tf_op jit(solution)/shard_map/all_to_all | solution.py:355
  26.0 1.3 shard_map.114
  27.3 1.9 %collective-permute-start = (bf16[16,128,128]{2,1,0:T(8,128)(2,1)S(1)}, bf16[16,128,128]{2,1,0:T(8,128)(2,1)S(1)}, u32[]{:S(2)}, u32[]{:S(2)}) collective-permute-start(bf16[16,128,128]{2,1,0:T(8,128)(2,1)S(1)} %get-tuple-element.13), channel_id=1, source_target_pairs={{0,1},{1,2},{2,3},{3,4},{4,5},{5,6},{6,7},{7,8},{8,9},{9,10},{10,1... | collective-permute-start | bytes 1572872 | tf_op jit(solution)/shard_map/ppermute | solution.py:37
  29.3 7.6 %collective-permute-start.1 = (bf16[16,128,128]{2,1,0:T(8,128)(2,1)S(1)}, bf16[16,128,128]{2,1,0:T(8,128)(2,1)S(1)}, u32[]{:S(2)}, u32[]{:S(2)}) collective-permute-start(bf16[16,128,128]{2,1,0:T(8,128)(2,1)S(1)} %get-tuple-element.14), channel_id=1, source_target_pairs={{0,11},{1,0},{2,1},{3,2},{4,3},{5,4},{6,5},{7,6},{8,7},{9,8},{10,9... | collective-permute-start | bytes 1572872 | tf_op jit(solution)/shard_map/ppermute | solution.py:37
  36.9 0.9 shard_map.113
  37.8 0.0 copy-start.1
  37.8 0.0 copy-start.2
  37.8 0.0 copy-start.4
  37.8 8.2 %collective-permute-done = bf16[16,128,128]{2,1,0:T(8,128)(2,1)S(1)} collective-permute-done((bf16[16,128,128]{2,1,0:T(8,128)(2,1)S(1)}, bf16[16,128,128]{2,1,0:T(8,128)(2,1)S(1)}, u32[]{:S(2)}, u32[]{:S(2)}) %collective-permute-start) | collective-permute-done | bytes 524320 | tf_op jit(solution)/shard_map/ppermute | solution.py:37
  46.1 0.9 collective-permute-done.1
  46.9 0.2 fusion.1
  47.1 27.9 %all_to_all.30.parts_ref = bf16[16,128,128]{2,1,0:T(8,128)(2,1)S(1)} all-to-all(bf16[16,128,128]{2,1,0:T(8,128)(2,1)S(1)} %fusion.1), channel_id=1, replica_groups=mesh['yl'=2,'x'=4,'core'=2,'yh'=4,'za'=4,'zb'=3] {'yh','za'}, dimensions={0} | all-to-all | bytes 1048576 | tf_op jit(solution)/shard_map/all_to_all | solution.py:361
  75.0 0.0 copy-done.1
  75.0 0.0 copy-done.2
  75.0 0.0 copy-done.4
  75.0 0.9 shard_map.115
  75.9 20.6 %all_to_all.31.grads_ref = f32[16,24,128]{2,1,0:T(8,128)S(1)} all-to-all(f32[16,24,128]{2,1,0:T(8,128)S(1)} %get-tuple-element.17), channel_id=1, replica_groups=mesh['yl'=2,'x'=4,'core'=2,'yh'=4,'za'=4,'zb'=3] {'yl','x','core'}, dimensions={0} | all-to-all | bytes 393216 | tf_op jit(solution)/shard_map/all_to_all | solution.py:363
  96.5 12.2 %all_to_all.32.parts_ref = bf16[4,160,128]{2,1,0:T(8,128)(2,1)S(1)} all-to-all(bf16[4,160,128]{2,1,0:T(8,128)(2,1)S(1)} %shard_map.116), channel_id=1, replica_groups=mesh['yl'=2,'x'=4,'core'=2,'yh'=4,'za'=4,'zb'=3] {'za'}, dimensions={0} | all-to-all | bytes 327680 | tf_op jit(solution)/shard_map/all_to_all | solution.py:364
  108.7 0.1 shard_map.117
  108.8 15.9 %all_to_all.33.parts_ref = bf16[4,544,128]{2,1,0:T(8,128)(2,1)S(1)} all-to-all(bf16[4,544,128]{2,1,0:T(8,128)(2,1)S(1)} %shard_map.117), channel_id=1, replica_groups=mesh['yl'=2,'x'=4,'core'=2,'yh'=4,'za'=4,'zb'=3] {'yh'}, dimensions={0} | all-to-all | bytes 1114112 | tf_op jit(solution)/shard_map/all_to_all | solution.py:365
  124.7 7.7 %collective-permute-start.3 = (bf16[2080,128]{1,0:T(8,128)(2,1)S(1)}, bf16[2080,128]{1,0:T(8,128)(2,1)S(1)}, u32[]{:S(2)}, u32[]{:S(2)}) collective-permute-start(bf16[2080,128]{1,0:T(8,128)(2,1)S(1)} %shard_map.118.panel_ref.refs_0_), channel_id=1, source_target_pairs={{0,1},{1,2},{2,3},{3,4},{4,5},{5,6},{6,7},{7,8},{8,9},{9,10},{10,1... | collective-permute-start | bytes 1597448 | tf_op jit(solution)/shard_map/ppermute | solution.py:37
  132.4 1.9 %collective-permute-start.2 = (bf16[2080,128]{1,0:T(8,128)(2,1)S(1)}, bf16[2080,128]{1,0:T(8,128)(2,1)S(1)}, u32[]{:S(2)}, u32[]{:S(2)}) collective-permute-start(bf16[2080,128]{1,0:T(8,128)(2,1)S(1)} %shard_map.118.panel_ref.refs_0_), channel_id=1, source_target_pairs={{0,11},{1,0},{2,1},{3,2},{4,3},{5,4},{6,5},{7,6},{8,7},{9,8},{10,9... | collective-permute-start | bytes 1597448 | tf_op jit(solution)/shard_map/ppermute | solution.py:37
  134.4 0.9 shard_map.119.refs_3_
  135.3 4.7 %collective-permute-done.3.refs_2_ = bf16[2080,128]{1,0:T(8,128)(2,1)S(1)} collective-permute-done((bf16[2080,128]{1,0:T(8,128)(2,1)S(1)}, bf16[2080,128]{1,0:T(8,128)(2,1)S(1)}, u32[]{:S(2)}, u32[]{:S(2)}) %collective-permute-start.3) | collective-permute-done | bytes 532512 | tf_op jit(solution)/shard_map/ppermute | solution.py:37
  140.0 2.8 %collective-permute-done.2.refs_1_ = bf16[2080,128]{1,0:T(8,128)(2,1)S(1)} collective-permute-done((bf16[2080,128]{1,0:T(8,128)(2,1)S(1)}, bf16[2080,128]{1,0:T(8,128)(2,1)S(1)}, u32[]{:S(2)}, u32[]{:S(2)}) %collective-permute-start.2) | collective-permute-done | bytes 532512 | tf_op jit(solution)/shard_map/ppermute | solution.py:37
  142.7 1.8 %shard_map.120 = (bf16[16,144,128]{2,1,0:T(8,128)(2,1)S(1)}, f32[1,256]{1,0:T(1,128)}) custom-call(s32[3,72]{1,0:T(4,128)S(1)} %multiply_reduce_fusion.order_ref, s32[4]{0:T(128)S(1)} %convert_reduce_fusion.1.ends_ref, s32[3]{0:T(128)S(1)} %and_select_fusion.index_ref, bf16[64,128,128]{2,1,0:T(8,128)(2,1)S(1)} %shard_map.111.values_ref, ...), custom_call_target="tpu_custom_call" | custom-call | tf_op jit(solution)/shard_map/pallas_call | solution.py:291
  144.5 24.7 %all_to_all.34.parts_ref = bf16[16,144,128]{2,1,0:T(8,128)(2,1)S(1)} all-to-all(bf16[16,144,128]{2,1,0:T(8,128)(2,1)S(1)} %get-tuple-element.18), channel_id=1, replica_groups=mesh['yl'=2,'x'=4,'core'=2,'yh'=4,'za'=4,'zb'=3] {'yl','x','core'}, dimensions={0} | all-to-all | bytes 1179648 | tf_op jit(solution)/shard_map/all_to_all | solution.py:372
  169.2 0.8 shard_map.121
  (7 shorter events, 0.1 us)
Async XLA Ops:
  0.6 0.8 copy-start.3
  1.4 14.8 %copy-start.5 = (s32[1,1,64]{2,1,0:T(1,128)S(1)}, s32[1,1,64]{2,1,0:T(1,128)}, u32[]{:S(2)}) copy-start(s32[1,1,64]{2,1,0:T(1,128)} %param.12) | copy-start | bytes 772
  1.4 14.8 %copy-start.6 = (s32[1,1,64]{2,1,0:T(1,128)S(1)}, s32[1,1,64]{2,1,0:T(1,128)}, u32[]{:S(2)}) copy-start(s32[1,1,64]{2,1,0:T(1,128)} %param.13) | copy-start | bytes 772
  2.3 23.8 %all-to-all-start = ((bf16[16,128,128]{2,1,0:T(8,128)(2,1)}), bf16[16,128,128]{2,1,0:T(8,128)(2,1)S(1)}, u32[]{:S(2)}, u32[]{:S(2)}) async-start(bf16[16,128,128]{2,1,0:T(8,128)(2,1)} %shard_map.112), calls=%async_computation | async-start | bytes 1048576 | tf_op jit(solution)/shard_map/all_to_all | solution.py:355
  16.9 1.6 copy-start
  27.3 18.7 %collective-permute-start = (bf16[16,128,128]{2,1,0:T(8,128)(2,1)S(1)}, bf16[16,128,128]{2,1,0:T(8,128)(2,1)S(1)}, u32[]{:S(2)}, u32[]{:S(2)}) collective-permute-start(bf16[16,128,128]{2,1,0:T(8,128)(2,1)S(1)} %get-tuple-element.13), channel_id=1, source_target_pairs={{0,1},{1,2},{2,3},{3,4},{4,5},{5,6},{6,7},{7,8},{8,9},{9,10},{10,1... | collective-permute-start | bytes 1572872 | tf_op jit(solution)/shard_map/ppermute | solution.py:37
  29.3 17.7 %collective-permute-start.1 = (bf16[16,128,128]{2,1,0:T(8,128)(2,1)S(1)}, bf16[16,128,128]{2,1,0:T(8,128)(2,1)S(1)}, u32[]{:S(2)}, u32[]{:S(2)}) collective-permute-start(bf16[16,128,128]{2,1,0:T(8,128)(2,1)S(1)} %get-tuple-element.14), channel_id=1, source_target_pairs={{0,11},{1,0},{2,1},{3,2},{4,3},{5,4},{6,5},{7,6},{8,7},{9,8},{10,9... | collective-permute-start | bytes 1572872 | tf_op jit(solution)/shard_map/ppermute | solution.py:37
  37.8 37.2 %copy-start.1 = (bf16[128,256]{1,0:T(8,128)(2,1)S(1)}, bf16[128,256]{1,0:T(8,128)(2,1)}, u32[]{:S(2)}) copy-start(bf16[128,256]{1,0:T(8,128)(2,1)} %cot_ref.1) | copy-start | bytes 196612
  37.8 37.2 %copy-start.2 = (bf16[128,256]{1,0:T(8,128)(2,1)S(1)}, bf16[128,256]{1,0:T(8,128)(2,1)}, u32[]{:S(2)}) copy-start(bf16[128,256]{1,0:T(8,128)(2,1)} %weight_ref.1) | copy-start | bytes 196612
  37.8 37.2 %copy-start.4 = (f32[256]{0:T(256)S(1)}, f32[256]{0:T(256)}, u32[]{:S(2)}) copy-start(f32[256]{0:T(256)} %param.10) | copy-start | bytes 3076
  124.7 15.3 %collective-permute-start.3 = (bf16[2080,128]{1,0:T(8,128)(2,1)S(1)}, bf16[2080,128]{1,0:T(8,128)(2,1)S(1)}, u32[]{:S(2)}, u32[]{:S(2)}) collective-permute-start(bf16[2080,128]{1,0:T(8,128)(2,1)S(1)} %shard_map.118.panel_ref.refs_0_), channel_id=1, source_target_pairs={{0,1},{1,2},{2,3},{3,4},{4,5},{5,6},{6,7},{7,8},{8,9},{9,10},{10,1... | collective-permute-start | bytes 1597448 | tf_op jit(solution)/shard_map/ppermute | solution.py:37
  132.4 10.3 %collective-permute-start.2 = (bf16[2080,128]{1,0:T(8,128)(2,1)S(1)}, bf16[2080,128]{1,0:T(8,128)(2,1)S(1)}, u32[]{:S(2)}, u32[]{:S(2)}) collective-permute-start(bf16[2080,128]{1,0:T(8,128)(2,1)S(1)} %shard_map.118.panel_ref.refs_0_), channel_id=1, source_target_pairs={{0,11},{1,0},{2,1},{3,2},{4,3},{5,4},{6,5},{7,6},{8,7},{9,8},{10,9... | collective-permute-start | bytes 1597448 | tf_op jit(solution)/shard_map/ppermute | solution.py:37

commit v5 on v3

--- a/solution.py
+++ b/solution.py
@@ -59,43 +59,32 @@
     slot_loop(order_ref, ends_ref[stage], ends_ref[stage + 1], add)
 
 
-def outer_kernel(order_ref, ends_ref, values_ref, panel_ref, *refs):
-    next_ref, back_ref, up_ref, down_ref, acc_ref = refs
+def near_kernel(order_ref, ends_ref, values_ref, panel_ref, next_ref, back_ref, acc_ref):
     acc_ref[...] = jnp.zeros_like(acc_ref)
-    trash = 3 * FAR
-    for stage in range(1, STAGES):
-        base = (min(stage, 3) - 1) * FAR
-        forward_slots(stage, base, trash, order_ref, ends_ref, values_ref, panel_ref, acc_ref)
+    for stage in (1, 2):
+        base = (stage - 1) * FAR
+        forward_slots(stage, base, 2 * FAR, order_ref, ends_ref, values_ref, panel_ref, acc_ref)
     next_ref[...] = acc_ref[:FAR].astype(jnp.bfloat16)
     back_ref[...] = acc_ref[FAR : 2 * FAR].astype(jnp.bfloat16)
-    up_ref[...] = acc_ref[2 * FAR : 2 * FAR + HALF].astype(jnp.bfloat16)
-    down_ref[...] = acc_ref[2 * FAR + HALF : 3 * FAR].astype(jnp.bfloat16)
-
-
-def forward_outer(order, ends, values, panel):
-    whole = jax.ShapeDtypeStruct((FAR, TILE, FIN), jnp.bfloat16)
-    half = jax.ShapeDtypeStruct((HALF, TILE, FIN), jnp.bfloat16)
-    return pl.pallas_call(
-        outer_kernel,
-        out_shape=(whole, whole, half, half),
+
+
+def rest_kernel(order_ref, ends_ref, values_ref, panel_ref, up_ref, down_ref, own_ref, acc_ref):
+    own_ref[...] = jnp.zeros_like(own_ref)
+    acc_ref[...] = jnp.zeros_like(acc_ref)
+    for stage in (3, 4):
+        forward_slots(stage, 0, FAR, order_ref, ends_ref, values_ref, panel_ref, acc_ref)
+    up_ref[...] = acc_ref[:HALF].astype(jnp.bfloat16)
+    down_ref[...] = acc_ref[HALF:FAR].astype(jnp.bfloat16)
+    forward_slots(0, 0, FAR, order_ref, ends_ref, values_ref, panel_ref, own_ref)
+
+
+def forward(kernel, shapes, tiles, order, ends, values, panel):
+    return pl.pallas_call(
+        kernel,
+        out_shape=shapes,
         in_specs=[SMEM, SMEM, VMEM, VMEM],
-        out_specs=(VMEM,) * 4,
-        scratch_shapes=[pltpu.VMEM((3 * FAR + 1, TILE, FIN), jnp.float32)],
-        compiler_params=LIMIT,
-    )(order, ends, values, panel)
-
-
-def inner_kernel(order_ref, ends_ref, values_ref, panel_ref, acc_ref):
-    acc_ref[...] = jnp.zeros_like(acc_ref)
-    forward_slots(0, 0, FAR, order_ref, ends_ref, values_ref, panel_ref, acc_ref)
-
-
-def forward_inner(order, ends, values, panel):
-    return pl.pallas_call(
-        inner_kernel,
-        out_shape=jax.ShapeDtypeStruct((FAR + 1, TILE, FIN), jnp.float32),
-        in_specs=[SMEM, SMEM, VMEM, VMEM],
-        out_specs=VMEM,
+        out_specs=(VMEM,) * len(shapes),
+        scratch_shapes=[pltpu.VMEM((tiles + 1, TILE, FIN), jnp.float32)],
         compiler_params=LIMIT,
     )(order, ends, values, panel)
 
@@ -254,10 +243,16 @@
     backward_slots(0, order_ref, ends_ref, values_ref, panel_ref, acc_ref)
 
 
+def middle_kernel(order_ref, ends_ref, values_ref, next_ref, back_ref, old_ref, acc_ref):
+    acc_ref[...] = old_ref[...]
+    backward_slots(1, order_ref, ends_ref, values_ref, next_ref, acc_ref)
+    backward_slots(2, order_ref, ends_ref, values_ref, back_ref, acc_ref)
+
+
 def last_kernel(factor, order_ref, ends_ref, index_ref, values_ref, *refs):
     panels, old_ref, out_ref, bgrad_ref, acc_ref, shares_ref = refs[:STAGES], *refs[STAGES:]
     acc_ref[...] = old_ref[...]
-    for stage in range(1, STAGES):
+    for stage in (3, 4):
         backward_slots(stage, order_ref, ends_ref, values_ref, panels[stage], acc_ref)
     out_ref[:, :TILE, :] = acc_ref[:CT].astype(jnp.bfloat16)
     middle = HALF * TILE
@@ -284,6 +279,16 @@
         out_specs=VMEM,
         compiler_params=LIMIT,
     )(order, ends, values, panel)
+
+
+def backward_middle(order, ends, values, panels, old):
+    return pl.pallas_call(
+        middle_kernel,
+        out_shape=ACC,
+        in_specs=[SMEM, SMEM] + [VMEM] * 4,
+        out_specs=VMEM,
+        compiler_params=LIMIT,
+    )(order, ends, values, *panels, old)
 
 
 def backward_last(factor, order, ends, index, values, panels, old):
@@ -354,10 +359,15 @@
     zone = lax.axis_index("zb")
     order, ends = slot_order(rows, cols, tile_count[0, 0], zone)
     panel = lax.all_to_all(repeat(features), ROW, 0, 0, tiled=True)
-    to_next, to_back, to_up, to_down = forward_outer(order, ends, values, panel)
+    whole = jax.ShapeDtypeStruct((FAR, TILE, FIN), jnp.bfloat16)
+    half = jax.ShapeDtypeStruct((HALF, TILE, FIN), jnp.bfloat16)
+    own = jax.ShapeDtypeStruct((FAR + 1, TILE, FIN), jnp.float32)
+    slots = (order, ends, values, panel)
+    to_next, to_back = forward(near_kernel, (whole, whole), 2 * FAR, *slots)
     arrived = (shift(to_next, 1), shift(to_back, -1))
+    to_up, to_down, own = forward(rest_kernel, (half, half, own), FAR, *slots)
     arrived += (jnp.concatenate([shift(to_up, 2), shift(to_down, -2)], axis=0),)
-    summed = forward_inner(order, ends, values, panel)[:FAR]
+    summed = own[:FAR]
     for part in arrived:
         summed = summed + part.astype(jnp.float32)
     parts = lax.all_to_all(summed.astype(jnp.bfloat16), GROUP, 0, 0, tiled=True)
@@ -367,6 +377,7 @@
     panel, up, down = join(targets)
     panels = [panel, shift(panel, -1), shift(panel, 1), shift(up, 2), shift(down, -2)]
     acc = backward_first(order, ends, values, panel)
+    acc = backward_middle(order, ends, values, panels[1:3], acc)
     index = jnp.remainder(jnp.arange(NEAR, dtype=jnp.int32) - zone, NEAR)
     factor = 1.0 / math.sqrt(TILE * lax.axis_size(ROW) * lax.axis_size(COL))
     back, bias_grad = backward_last(factor, order, ends, index, values, panels, acc)

time: 169 us -> 169 us (level)
  blocking collectives: 86.1 us -> 79.1 us
  starting transfers between devices: 44.5 us -> 49.9 us
  Pallas kernels: 9.23 us -> 11.2 us
    ppermute x8, starting transfers between devices: 30.6 us -> 36 us  [shift(): lax.ppermute(block, LINE, [(z, (z + steps) % DEPTH) for z in range(DEPTH)])]
    all_to_all x1, blocking collectives: 28.1 us -> 23.7 us  [local(): targets = lax.all_to_all(spread(proj, grads), GROUP, 0, 0, tiled=True)]
    pallas_call x2 -> x3, Pallas kernels: 2.91 us -> 5.18 us  [the longest x2 3.6 us: forward(): pl.pallas_call(kernel, out_shape=shapes, in_specs=[SMEM, SMEM, VMEM, VMEM...]
  transfers between devices with their start and end apart: 9 -> 9, of which waited for: 5 -> 6; matrix products, arithmetic and copies ran while one was open for 1% -> 1% of each run, Pallas kernels for 1% -> 3%
where the time goes in v5:
time: 169 us; the launch traced here: 168 us
  blocking collectives  79.1 us (47%)
  starting transfers between devices  49.9 us (30%)
  waiting for transfers between devices  22.4 us (13%)
  Pallas kernels  11.2 us (7%)
  local copies, waits for them, and re-layouts  2.75 us (2%)
    ppermute x8, starting transfers between devices, shift(): lax.ppermute(block, LINE, [(z, (z + steps) % DEPTH) for z in range(DEPTH)])  36 us
    all_to_all x1, blocking collectives, local(): parts = lax.all_to_all(summed.astype(jnp.bfloat16), GROUP, 0, 0, tiled=True)  25.8 us
    all_to_all x1, blocking collectives, local(): targets = lax.all_to_all(spread(proj, grads), GROUP, 0, 0, tiled=True)  23.7 us
    ppermute x8, waiting for transfers between devices, shift(): lax.ppermute(block, LINE, [(z, (z + steps) % DEPTH) for z in range(DEPTH)])  16.6 us
    all_to_all x1, blocking collectives, local(): back = lax.all_to_all(back, ROW, 0, 0, tiled=True)  15.6 us
    all_to_all x1, blocking collectives, local(): grads = lax.all_to_all(grads, ROW, 0, 0, tiled=True)  14 us
    all_to_all x1, starting transfers between devices, local(): panel = lax.all_to_all(repeat(features), ROW, 0, 0, tiled=True)  13.9 us
    all_to_all x1, waiting for transfers between devices, local(): panel = lax.all_to_all(repeat(features), ROW, 0, 0, tiled=True)  5.79 us
  transfers between devices with their start and end apart: 9, of which 6 were waited for; matrix products, arithmetic and copies ran while one was open for 1% of the time, Pallas kernels for 3%

profile of v5, /device:TPU:1, one launch (start us, length us, event | category | flops | bytes accessed | tf_op | source)
XLA Modules:
  0.0 168.3 jit_solution(1184893556664836706)
XLA Ops:
  0.6 0.0 copy-start.3
  0.6 0.7 copy-done.3
  1.4 0.9 shard_map.112
  2.3 13.9 %all-to-all-start = ((bf16[16,128,128]{2,1,0:T(8,128)(2,1)}), bf16[16,128,128]{2,1,0:T(8,128)(2,1)S(1)}, u32[]{:S(2)}, u32[]{:S(2)}) async-start(bf16[16,128,128]{2,1,0:T(8,128)(2,1)} %shard_map.112), calls=%async_computation | async-start | bytes 1048576 | tf_op jit(solution)/shard_map/all_to_all | solution.py:361
  16.2 0.7 and_select_fusion.3
  17.5 0.0 copy-start
  17.5 1.6 copy-done
  19.1 0.2 shard_map.111.values_ref
  19.4 0.4 copy-done.5
  19.8 0.1 convert_reduce_fusion.1.ends_ref
  19.9 0.2 convert_reduce_fusion
  20.1 0.1 fusion
  20.1 0.1 multiply_reduce_fusion.order_ref
  20.3 5.8 %all-to-all-done.panel_ref = bf16[16,128,128]{2,1,0:T(8,128)(2,1)S(1)} async-done(((bf16[16,128,128]{2,1,0:T(8,128)(2,1)}), bf16[16,128,128]{2,1,0:T(8,128)(2,1)S(1)}, u32[]{:S(2)}, u32[]{:S(2)}) %all-to-all-start) | async-done | bytes 524320 | tf_op jit(solution)/shard_map/all_to_all | solution.py:361
  26.0 1.7 %shard_map.114 = (bf16[12,128,128]{2,1,0:T(8,128)(2,1)S(1)}, bf16[12,128,128]{2,1,0:T(8,128)(2,1)S(1)}) custom-call(s32[3,72]{1,0:T(4,128)S(1)} %multiply_reduce_fusion.order_ref, s32[6]{0:T(128)S(1)} %convert_reduce_fusion.1.ends_ref, bf16[64,128,128]{2,1,0:T(8,128)(2,1)S(1)} %shard_map.111.values_ref, bf16[16,128,128]{2,1,0:T(8,128)(2,1)S(1)} %all-to-all-done.panel_ref), custom_call_target="tpu_custom_call" | custom-call | tf_op jit(solution)/shard_map/pallas_call | solution.py:82
  27.7 1.9 %collective-permute-start = (bf16[12,128,128]{2,1,0:T(8,128)(2,1)S(1)}, bf16[12,128,128]{2,1,0:T(8,128)(2,1)S(1)}, u32[]{:S(2)}, u32[]{:S(2)}) collective-permute-start(bf16[12,128,128]{2,1,0:T(8,128)(2,1)S(1)} %get-tuple-element.20), channel_id=1, source_target_pairs={{0,1},{1,2},{2,3},{3,4},{4,5},{5,6},{6,7},{7,8},{8,9},{9,10},{10,1... | collective-permute-start | bytes 1179656 | tf_op jit(solution)/shard_map/ppermute | solution.py:37
  29.7 6.7 %collective-permute-start.1 = (bf16[12,128,128]{2,1,0:T(8,128)(2,1)S(1)}, bf16[12,128,128]{2,1,0:T(8,128)(2,1)S(1)}, u32[]{:S(2)}, u32[]{:S(2)}) collective-permute-start(bf16[12,128,128]{2,1,0:T(8,128)(2,1)S(1)} %get-tuple-element.21), channel_id=1, source_target_pairs={{0,11},{1,0},{2,1},{3,2},{4,3},{5,4},{6,5},{7,6},{8,7},{9,8},{10,9... | collective-permute-start | bytes 1179656 | tf_op jit(solution)/shard_map/ppermute | solution.py:37
  36.4 1.9 %shard_map.113 = (bf16[6,128,128]{2,1,0:T(8,128)(2,1)S(1)}, bf16[6,128,128]{2,1,0:T(8,128)(2,1)S(1)}, f32[13,128,128]{2,1,0:T(8,128)S(1)}) custom-call(s32[3,72]{1,0:T(4,128)S(1)} %multiply_reduce_fusion.order_ref, s32[6]{0:T(128)S(1)} %convert_reduce_fusion.1.ends_ref, bf16[64,128,128]{2,1,0:T(8,128)(2,1)S(1)} %shard_map.111.values_ref, ...), custom_call_target="tpu_custom_call" | custom-call | tf_op jit(solution)/shard_map/pallas_call | solution.py:82
  38.3 0.0 copy-start.1
  38.3 0.0 copy-start.2
  38.3 0.0 copy-start.4
  38.3 2.1 %collective-permute-start.2 = (bf16[6,128,128]{2,1,0:T(8,128)(2,1)S(1)}, bf16[6,128,128]{2,1,0:T(8,128)(2,1)S(1)}, u32[]{:S(2)}, u32[]{:S(2)}) collective-permute-start(bf16[6,128,128]{2,1,0:T(8,128)(2,1)S(1)} %get-tuple-element.22), channel_id=1, source_target_pairs={{0,2},{1,3},{2,4},{3,5},{4,6},{5,7},{6,8},{7,9},{8,10},{9,11},{10,... | collective-permute-start | bytes 589832 | tf_op jit(solution)/shard_map/ppermute | solution.py:37
  40.4 5.5 %collective-permute-start.3 = (bf16[6,128,128]{2,1,0:T(8,128)(2,1)S(1)}, bf16[6,128,128]{2,1,0:T(8,128)(2,1)S(1)}, u32[]{:S(2)}, u32[]{:S(2)}) collective-permute-start(bf16[6,128,128]{2,1,0:T(8,128)(2,1)S(1)} %get-tuple-element.23), channel_id=1, source_target_pairs={{0,10},{1,11},{2,0},{3,1},{4,2},{5,3},{6,4},{7,5},{8,6},{9,7},{10,... | collective-permute-start | bytes 589832 | tf_op jit(solution)/shard_map/ppermute | solution.py:37
  45.9 5.0 %collective-permute-done.2 = bf16[6,128,128]{2,1,0:T(8,128)(2,1)S(1)} collective-permute-done((bf16[6,128,128]{2,1,0:T(8,128)(2,1)S(1)}, bf16[6,128,128]{2,1,0:T(8,128)(2,1)S(1)}, u32[]{:S(2)}, u32[]{:S(2)}) %collective-permute-start.2) | collective-permute-done | bytes 196640 | tf_op jit(solution)/shard_map/ppermute | solution.py:37
  50.9 2.7 %collective-permute-done.3 = bf16[6,128,128]{2,1,0:T(8,128)(2,1)S(1)} collective-permute-done((bf16[6,128,128]{2,1,0:T(8,128)(2,1)S(1)}, bf16[6,128,128]{2,1,0:T(8,128)(2,1)S(1)}, u32[]{:S(2)}, u32[]{:S(2)}) %collective-permute-start.3) | collective-permute-done | bytes 196640 | tf_op jit(solution)/shard_map/ppermute | solution.py:37
  53.6 0.0 collective-permute-done
  53.6 0.0 collective-permute-done.1
  53.6 0.2 add_convert_fusion
  53.8 25.8 %all_to_all.25.parts_ref = bf16[12,128,128]{2,1,0:T(8,128)(2,1)S(1)} all-to-all(bf16[12,128,128]{2,1,0:T(8,128)(2,1)S(1)} %add_convert_fusion), channel_id=1, replica_groups=mesh['yl'=2,'x'=4,'core'=2,'yh'=4,'za'=3,'zb'=4] {'yh','za'}, dimensions={0} | all-to-all | bytes 786432 | tf_op jit(solution)/shard_map/all_to_all | solution.py:373
  79.6 0.0 copy-done.1
  79.6 0.9 shard_map.115
  80.5 14.0 %all_to_all.26.grads_ref = f32[16,24,128]{2,1,0:T(8,128)S(1)} all-to-all(f32[16,24,128]{2,1,0:T(8,128)S(1)} %get-tuple-element.26), channel_id=1, replica_groups=mesh['yl'=2,'x'=4,'core'=2,'yh'=4,'za'=3,'zb'=4] {'yl','x','core'}, dimensions={0} | all-to-all | bytes 393216 | tf_op jit(solution)/shard_map/all_to_all | solution.py:375
  94.4 0.1 shard_map.116
  94.5 23.7 %all_to_all.27.parts_ref = bf16[12,160,128]{2,1,0:T(8,128)(2,1)S(1)} all-to-all(bf16[12,160,128]{2,1,0:T(8,128)(2,1)S(1)} %shard_map.116), channel_id=1, replica_groups=mesh['yl'=2,'x'=4,'core'=2,'yh'=4,'za'=3,'zb'=4] {'yh','za'}, dimensions={0} | all-to-all | bytes 983040 | tf_op jit(solution)/shard_map/all_to_all | solution.py:376
  118.2 0.1 shard_map.117
  118.4 3.3 %collective-permute-start.5 = (bf16[1568,128]{1,0:T(8,128)(2,1)S(1)}, bf16[1568,128]{1,0:T(8,128)(2,1)S(1)}, u32[]{:S(2)}, u32[]{:S(2)}) collective-permute-start(bf16[1568,128]{1,0:T(8,128)(2,1)S(1)} %get-tuple-element.27.panel_ref.refs_0_), channel_id=1, source_target_pairs={{0,1},{1,2},{2,3},{3,4},{4,5},{5,6},{6,7},{7,8},{8,9},{9,10},{10,1... | collective-permute-start | bytes 1204232 | tf_op jit(solution)/shard_map/ppermute | solution.py:37
  121.7 9.1 %collective-permute-start.4 = (bf16[1568,128]{1,0:T(8,128)(2,1)S(1)}, bf16[1568,128]{1,0:T(8,128)(2,1)S(1)}, u32[]{:S(2)}, u32[]{:S(2)}) collective-permute-start(bf16[1568,128]{1,0:T(8,128)(2,1)S(1)} %get-tuple-element.27.panel_ref.refs_0_), channel_id=1, source_target_pairs={{0,11},{1,0},{2,1},{3,2},{4,3},{5,4},{6,5},{7,6},{8,7},{9,8},{10,9... | collective-permute-start | bytes 1204232 | tf_op jit(solution)/shard_map/ppermute | solution.py:37
  130.8 4.0 %collective-permute-start.6 = (bf16[800,128]{1,0:T(8,128)(2,1)S(1)}, bf16[800,128]{1,0:T(8,128)(2,1)S(1)}, u32[]{:S(2)}, u32[]{:S(2)}) collective-permute-start(bf16[800,128]{1,0:T(8,128)(2,1)S(1)} %get-tuple-element.28), channel_id=1, source_target_pairs={{0,2},{1,3},{2,4},{3,5},{4,6},{5,7},{6,8},{7,9},{8,10},{9,11},{10,... | collective-permute-start | bytes 614408 | tf_op jit(solution)/shard_map/ppermute | solution.py:37
  134.8 3.4 %collective-permute-start.7 = (bf16[800,128]{1,0:T(8,128)(2,1)S(1)}, bf16[800,128]{1,0:T(8,128)(2,1)S(1)}, u32[]{:S(2)}, u32[]{:S(2)}) collective-permute-start(bf16[800,128]{1,0:T(8,128)(2,1)S(1)} %get-tuple-element.29), channel_id=1, source_target_pairs={{0,10},{1,11},{2,0},{3,1},{4,2},{5,3},{6,4},{7,5},{8,6},{9,7},{10,... | collective-permute-start | bytes 614408 | tf_op jit(solution)/shard_map/ppermute | solution.py:37
  138.2 1.1 shard_map.118.old_ref
  139.4 0.0 collective-permute-done.5.back_ref.refs_2_
  139.4 0.9 collective-permute-done.4.next_ref.refs_1_
  140.2 1.6 shard_map.119.refs_5_
  141.8 2.0 %collective-permute-done.6.refs_3_ = bf16[800,128]{1,0:T(8,128)(2,1)S(1)} collective-permute-done((bf16[800,128]{1,0:T(8,128)(2,1)S(1)}, bf16[800,128]{1,0:T(8,128)(2,1)S(1)}, u32[]{:S(2)}, u32[]{:S(2)}) %collective-permute-start.6) | collective-permute-done | bytes 204832 | tf_op jit(solution)/shard_map/ppermute | solution.py:37
  143.8 6.1 %collective-permute-done.7.refs_4_ = bf16[800,128]{1,0:T(8,128)(2,1)S(1)} collective-permute-done((bf16[800,128]{1,0:T(8,128)(2,1)S(1)}, bf16[800,128]{1,0:T(8,128)(2,1)S(1)}, u32[]{:S(2)}, u32[]{:S(2)}) %collective-permute-start.7) | collective-permute-done | bytes 204832 | tf_op jit(solution)/shard_map/ppermute | solution.py:37
  149.9 2.0 %shard_map.120 = (bf16[16,144,128]{2,1,0:T(8,128)(2,1)S(1)}, f32[1,256]{1,0:T(1,128)}) custom-call(s32[3,72]{1,0:T(4,128)S(1)} %multiply_reduce_fusion.order_ref, s32[6]{0:T(128)S(1)} %convert_reduce_fusion.1.ends_ref, s32[4]{0:T(128)S(1)} %and_select_fusion.index_ref, bf16[64,128,128]{2,1,0:T(8,128)(2,1)S(1)} %shard_map.111.values_ref, ...), custom_call_target="tpu_custom_call" | custom-call | tf_op jit(solution)/shard_map/pallas_call | solution.py:295
  151.9 15.6 %all_to_all.28.parts_ref = bf16[16,144,128]{2,1,0:T(8,128)(2,1)S(1)} all-to-all(bf16[16,144,128]{2,1,0:T(8,128)(2,1)S(1)} %get-tuple-element.30), channel_id=1, replica_groups=mesh['yl'=2,'x'=4,'core'=2,'yh'=4,'za'=3,'zb'=4] {'yl','x','core'}, dimensions={0} | all-to-all | bytes 1179648 | tf_op jit(solution)/shard_map/all_to_all | solution.py:384
  167.5 0.8 shard_map.121
  (7 shorter events, 0.0 us)
Async XLA Ops:
  0.6 0.8 copy-start.3
  2.3 23.8 %all-to-all-start = ((bf16[16,128,128]{2,1,0:T(8,128)(2,1)}), bf16[16,128,128]{2,1,0:T(8,128)(2,1)S(1)}, u32[]{:S(2)}, u32[]{:S(2)}) async-start(bf16[16,128,128]{2,1,0:T(8,128)(2,1)} %shard_map.112), calls=%async_computation | async-start | bytes 1048576 | tf_op jit(solution)/shard_map/all_to_all | solution.py:361
  17.5 1.6 copy-start
  19.1 0.7 copy-start.5
  27.7 25.8 %collective-permute-start = (bf16[12,128,128]{2,1,0:T(8,128)(2,1)S(1)}, bf16[12,128,128]{2,1,0:T(8,128)(2,1)S(1)}, u32[]{:S(2)}, u32[]{:S(2)}) collective-permute-start(bf16[12,128,128]{2,1,0:T(8,128)(2,1)S(1)} %get-tuple-element.20), channel_id=1, source_target_pairs={{0,1},{1,2},{2,3},{3,4},{4,5},{5,6},{6,7},{7,8},{8,9},{9,10},{10,1... | collective-permute-start | bytes 1179656 | tf_op jit(solution)/shard_map/ppermute | solution.py:37
  29.7 23.9 %collective-permute-start.1 = (bf16[12,128,128]{2,1,0:T(8,128)(2,1)S(1)}, bf16[12,128,128]{2,1,0:T(8,128)(2,1)S(1)}, u32[]{:S(2)}, u32[]{:S(2)}) collective-permute-start(bf16[12,128,128]{2,1,0:T(8,128)(2,1)S(1)} %get-tuple-element.21), channel_id=1, source_target_pairs={{0,11},{1,0},{2,1},{3,2},{4,3},{5,4},{6,5},{7,6},{8,7},{9,8},{10,9... | collective-permute-start | bytes 1179656 | tf_op jit(solution)/shard_map/ppermute | solution.py:37
  38.3 41.3 %copy-start.1 = (bf16[128,256]{1,0:T(8,128)(2,1)S(1)}, bf16[128,256]{1,0:T(8,128)(2,1)}, u32[]{:S(2)}) copy-start(bf16[128,256]{1,0:T(8,128)(2,1)} %cot_ref.1) | copy-start | bytes 196612
  38.3 41.3 %copy-start.2 = (bf16[128,256]{1,0:T(8,128)(2,1)S(1)}, bf16[128,256]{1,0:T(8,128)(2,1)}, u32[]{:S(2)}) copy-start(bf16[128,256]{1,0:T(8,128)(2,1)} %weight_ref.1) | copy-start | bytes 196612
  38.3 41.2 %copy-start.4 = (f32[256]{0:T(256)S(1)}, f32[256]{0:T(256)}, u32[]{:S(2)}) copy-start(f32[256]{0:T(256)} %param.10) | copy-start | bytes 3076
  38.3 12.5 %collective-permute-start.2 = (bf16[6,128,128]{2,1,0:T(8,128)(2,1)S(1)}, bf16[6,128,128]{2,1,0:T(8,128)(2,1)S(1)}, u32[]{:S(2)}, u32[]{:S(2)}) collective-permute-start(bf16[6,128,128]{2,1,0:T(8,128)(2,1)S(1)} %get-tuple-element.22), channel_id=1, source_target_pairs={{0,2},{1,3},{2,4},{3,5},{4,6},{5,7},{6,8},{7,9},{8,10},{9,11},{10,... | collective-permute-start | bytes 589832 | tf_op jit(solution)/shard_map/ppermute | solution.py:37
  40.4 13.2 %collective-permute-start.3 = (bf16[6,128,128]{2,1,0:T(8,128)(2,1)S(1)}, bf16[6,128,128]{2,1,0:T(8,128)(2,1)S(1)}, u32[]{:S(2)}, u32[]{:S(2)}) collective-permute-start(bf16[6,128,128]{2,1,0:T(8,128)(2,1)S(1)} %get-tuple-element.23), channel_id=1, source_target_pairs={{0,10},{1,11},{2,0},{3,1},{4,2},{5,3},{6,4},{7,5},{8,6},{9,7},{10,... | collective-permute-start | bytes 589832 | tf_op jit(solution)/shard_map/ppermute | solution.py:37
  118.4 21.0 %collective-permute-start.5 = (bf16[1568,128]{1,0:T(8,128)(2,1)S(1)}, bf16[1568,128]{1,0:T(8,128)(2,1)S(1)}, u32[]{:S(2)}, u32[]{:S(2)}) collective-permute-start(bf16[1568,128]{1,0:T(8,128)(2,1)S(1)} %get-tuple-element.27.panel_ref.refs_0_), channel_id=1, source_target_pairs={{0,1},{1,2},{2,3},{3,4},{4,5},{5,6},{6,7},{7,8},{8,9},{9,10},{10,1... | collective-permute-start | bytes 1204232 | tf_op jit(solution)/shard_map/ppermute | solution.py:37
  121.7 18.5 %collective-permute-start.4 = (bf16[1568,128]{1,0:T(8,128)(2,1)S(1)}, bf16[1568,128]{1,0:T(8,128)(2,1)S(1)}, u32[]{:S(2)}, u32[]{:S(2)}) collective-permute-start(bf16[1568,128]{1,0:T(8,128)(2,1)S(1)} %get-tuple-element.27.panel_ref.refs_0_), channel_id=1, source_target_pairs={{0,11},{1,0},{2,1},{3,2},{4,3},{5,4},{6,5},{7,6},{8,7},{9,8},{10,9... | collective-permute-start | bytes 1204232 | tf_op jit(solution)/shard_map/ppermute | solution.py:37
  130.8 13.0 %collective-permute-start.6 = (bf16[800,128]{1,0:T(8,128)(2,1)S(1)}, bf16[800,128]{1,0:T(8,128)(2,1)S(1)}, u32[]{:S(2)}, u32[]{:S(2)}) collective-permute-start(bf16[800,128]{1,0:T(8,128)(2,1)S(1)} %get-tuple-element.28), channel_id=1, source_target_pairs={{0,2},{1,3},{2,4},{3,5},{4,6},{5,7},{6,8},{7,9},{8,10},{9,11},{10,... | collective-permute-start | bytes 614408 | tf_op jit(solution)/shard_map/ppermute | solution.py:37
  134.8 15.1 %collective-permute-start.7 = (bf16[800,128]{1,0:T(8,128)(2,1)S(1)}, bf16[800,128]{1,0:T(8,128)(2,1)S(1)}, u32[]{:S(2)}, u32[]{:S(2)}) collective-permute-start(bf16[800,128]{1,0:T(8,128)(2,1)S(1)} %get-tuple-element.29), channel_id=1, source_target_pairs={{0,10},{1,11},{2,0},{3,1},{4,2},{5,3},{6,4},{7,5},{8,6},{9,7},{10,... | collective-permute-start | bytes 614408 | tf_op jit(solution)/shard_map/ppermute | solution.py:37
